TPU v7x, 128 devices: a whole 4x4x4 slice. The times are simulated.
128 devices in a mesh: grp: 4 (over y), leaf: 32 (over x, z, core).
Axes of the slice: x: 4, y: 4, z: 4, core: 2. Of those that a mesh axis runs over, the one named last changes fastest.
Arguments:
- right_side: float32 [98304, 512], P(('grp', 'leaf')), may hold values from -6 to 6
- guess: float32 [98304, 512], P(('grp', 'leaf')), may hold values from -6 to 6
- near_diag: float32 [128, 768, 768], P(('grp', 'leaf')), as said below
- near_lower: float32 [128, 768, 768], P(('grp', 'leaf')), may hold values from -0.0546875 to 0.0546875
- near_upper: float32 [128, 768, 768], P(('grp', 'leaf')), may hold values from -0.0546875 to 0.0546875
- leaf_inverse: float32 [128, 768, 768], P(('grp', 'leaf')), as said below
- leaf_basis: float32 [128, 768, 128], P(('grp', 'leaf')), may hold values from -0.21875 to 0.21875
- leaf_transfer: float32 [128, 128, 128], P(('grp', 'leaf')), may hold values from -0.5 to 0.5
- mid_share: float32 [128, 128, 128], P(('grp', 'leaf')), may hold values from -0.25 to 0.25
- top_share: float32 [128, 128, 128], P(('grp', 'leaf')), may hold values from -0.09375 to 0.09375
- coupling_share: float32 [128, 3, 128, 128], P(('grp', 'leaf')), as said below
Outputs:
- new_guess: float32 [98304, 512], P(('grp', 'leaf'))
- new_residual: float32 [98304, 512], P(('grp', 'leaf'))
Inputs may be any that keep to these rules, and one draw needn't show every extreme that they name: `near_diag`: each leaf's block has a dominant diagonal near 2. `leaf_inverse`: each leaf's matrix is symmetric positive definite. `coupling_share`: every share is symmetric, and each sum of shares that forms a coupling is positive definite.
All inputs are finite; a program needn't handle non-finite values.
Results may differ from a plain program's by a relative error of at most 0.00005.
Values sent between devices are 32-bit elements; how exact they have to be, the bound alone decides.
A program may use at most 128 MiB of HBM per device.

v0:
```python
import jax
import jax.numpy as jnp
from jax import lax
from jax.sharding import PartitionSpec as P

highest = lax.Precision.HIGHEST


def with_halo(block, sides, width):
    for axis, dim in sides:
        count = lax.axis_size(axis)
        forward = [(i, i + 1) for i in range(count - 1)]
        backward = [(target, source) for source, target in forward]
        low = lax.ppermute(
            lax.slice_in_dim(block, block.shape[dim] - width, None, axis=dim), axis, forward
        )
        high = lax.ppermute(lax.slice_in_dim(block, 0, width, axis=dim), axis, backward)
        block = jnp.concatenate([low, block, high], axis=dim)
    return block


def from_partner(value, axis, stride):
    mask = 2**stride
    pairs = [(source, source ^ mask) for source in range(lax.axis_size(axis))]
    return lax.ppermute(value, axis, pairs)


def product(left, right):
    return jnp.einsum("...kl,...lr->...kr", left, right, precision=highest)


def across(left, right):
    return jnp.einsum("...kl,...kr->...lr", left, right, precision=highest)


def definite_solve(matrix, target):
    factor = jnp.linalg.cholesky(matrix)
    halfway = lax.linalg.triangular_solve(factor, target, left_side=True, lower=True)
    return lax.linalg.triangular_solve(
        factor, halfway, left_side=True, lower=True, transpose_a=True
    )


def near_apply(blocks, diagonal, lower_block, upper_block):
    length = blocks.shape[0]
    padded = with_halo(blocks, ((("grp", "leaf"), 0),), length)
    result = product(diagonal, blocks)
    result = result + product(lower_block, padded[:length])
    return result + product(upper_block, padded[2 * length :])


def body(
    right_side,
    guess,
    near_diag,
    near_lower,
    near_upper,
    leaf_inverse,
    leaf_basis,
    leaf_transfer,
    mid_share,
    top_share,
    coupling_share,
):
    diagonal = near_diag[0]
    lower_block = near_lower[0]
    upper_block = near_upper[0]
    inverse = leaf_inverse[0]
    basis = leaf_basis[0]
    transfer = leaf_transfer[0]
    shares = coupling_share[0]
    residual = right_side - near_apply(guess, diagonal, lower_block, upper_block)
    weighted = product(inverse, basis)
    leaf_schur = across(basis, weighted)
    block_proj = across(transfer, product(leaf_schur, transfer))
    block_coup = shares[0]
    block_mid = mid_share[0]
    for bit_index in range(2):
        partner = from_partner((block_proj, block_coup, block_mid), "leaf", bit_index)
        block_proj = block_proj + partner[0]
        block_coup = block_coup + partner[1]
        block_mid = block_mid + partner[2]
    block_sys = block_coup + block_proj
    block_fix = definite_solve(block_sys, block_proj)
    block_schur = block_proj - product(block_proj, block_fix)
    leader = (lax.axis_index("leaf") % 4 == 0).astype(jnp.float32)
    group_sums = lax.psum(
        (
            leader * across(block_mid, product(block_schur, block_mid)),
            shares[1],
            top_share[0],
            shares[2],
        ),
        "leaf",
    )
    group_proj = group_sums[0]
    group_top = group_sums[2]
    group_sys = group_sums[1] + group_proj
    group_schur = group_proj - product(group_proj, definite_solve(group_sys, group_proj))
    root_sums = lax.psum((across(group_top, product(group_schur, group_top)), group_sums[3]), "grp")
    root_sys = root_sums[1] + root_sums[0]
    local_sol = product(inverse, residual)
    leaf_terms = across(transfer, across(basis, local_sol))
    block_rhs = leaf_terms
    for bit_index in range(2):
        block_rhs = block_rhs + from_partner(block_rhs, "leaf", bit_index)
    block_red = block_rhs - product(block_proj, definite_solve(block_sys, block_rhs))
    group_rhs = lax.psum(leader * across(block_mid, block_red), "leaf")
    group_red = group_rhs - product(group_proj, definite_solve(group_sys, group_rhs))
    root_rhs = lax.psum(across(group_top, group_red), "grp")
    root_t = definite_solve(root_sys, root_rhs)
    group_in = product(group_top, root_t)
    group_out = group_in + definite_solve(group_sys, group_rhs - product(group_proj, group_in))
    block_in = product(block_mid, group_out)
    block_out = block_in + definite_solve(block_sys, block_rhs - product(block_proj, block_in))
    leaf_in = product(transfer, block_out)
    new_guess = guess + (local_sol - product(weighted, leaf_in))
    new_residual = right_side - near_apply(new_guess, diagonal, lower_block, upper_block)
    return (new_guess, new_residual)


def solution(mesh):
    in_specs = (
        P(("grp", "leaf"), None),
        P(("grp", "leaf"), None),
        P(("grp", "leaf"), None, None),
        P(("grp", "leaf"), None, None),
        P(("grp", "leaf"), None, None),
        P(("grp", "leaf"), None, None),
        P(("grp", "leaf"), None, None),
        P(("grp", "leaf"), None, None),
        P(("grp", "leaf"), None, None),
        P(("grp", "leaf"), None, None),
        P(("grp", "leaf"), None, None, None),
    )
    out_specs = (P(("grp", "leaf"), None), P(("grp", "leaf"), None))
    return jax.shard_map(body, mesh=mesh, in_specs=in_specs, out_specs=out_specs, check_vma=False)
```

profile of v0, /device:TPU:16, one launch (start us, length us, event | category | flops | bytes accessed | tf_op | source)
XLA Modules:
  0.0 369.4 jit_solution(12311830670466724527)
XLA Ops:
  9.3 7.9 %collective-permute-start.1 = (f32[768,512]{1,0:T(8,128)}, f32[768,512]{1,0:T(8,128)}, u32[]{:S(2)}, u32[]{:S(2)}) collective-permute-start(f32[768,512]{1,0:T(8,128)} %param.21), channel_id=1, source_target_pairs={{1,0},{2,1},{3,2},{4,3},{5,4},{6,5},{7,6},{8,7},{9,8},{10,9},{11,1... | collective-permute-start | bytes 4718600 | tf_op jit(solution)/shard_map/ppermute | solution.py:17
  18.3 3.8 %fusion = f32[768,128]{1,0:T(8,128)S(1)} fusion(f32[1,768,768]{2,1,0:T(8,128)} %param.25, f32[1,768,128]{2,1,0:T(8,128)} %param.26), kind=kOutput, calls=%fused_computation | convolution fusion | flops 905969664 | bytes 3145728 | tf_op jit(solution)/shard_map/...kl,...lr->...kr/dot_general | solution.py:29
  24.2 5.0 %fusion.14 = f32[768,512]{1,0:T(8,128)} fusion(f32[768,512]{1,0:T(8,128)S(1)} %copy-done.10, f32[1,768,768]{2,1,0:T(8,128)S(1)} %copy-done), kind=kOutput, calls=%fused_computation.14 | convolution fusion | flops 3623878656 | bytes 5505024 | tf_op jit(solution)/shard_map/...kl,...lr->...kr/dot_general | solution.py:29
  38.1 12.5 %cholesky.59 = f32[128,128]{1,0:T(8,128)S(1)} custom-call(f32[128,128]{1,0:T(8,128)} %fusion.59), custom_call_target="Cholesky" | custom-call | tf_op jit(solution)/shard_map/jit(cholesky)/cholesky | solution.py:37
  52.0 9.8 %custom-call.25 = f32[1,128,128]{1,2,0:T(8,128)S(1)} custom-call(f32[1,128,128]{2,1,0:T(8,128)S(1)} %fusion.28), custom_call_target="InvertDiagBlocksLowerTriangular" | custom-call | tf_op jit(solution)/shard_map/triangular_solve/custom-call.2 | solution.py:39
  62.1 6.1 %fusion.10 = f32[768,512]{1,0:T(8,128)S(1)} fusion(f32[768,512]{1,0:T(8,128)} %collective-permute-done, f32[1,768,768]{2,1,0:T(8,128)} %param.23), kind=kOutput, calls=%fused_computation.10 | convolution fusion | flops 3623878656 | bytes 5505024 | tf_op jit(solution)/shard_map/...kl,...lr->...kr/dot_general | solution.py:29
  68.3 5.9 %fusion.6 = f32[768,512]{1,0:T(8,128)S(1)} fusion(f32[768,512]{1,0:T(8,128)} %collective-permute-done.1, f32[1,768,768]{2,1,0:T(8,128)S(1)} %copy-done.4), kind=kOutput, calls=%fused_computation.6 | convolution fusion | flops 3623878656 | bytes 5505024 | tf_op jit(solution)/shard_map/...kl,...lr->...kr/dot_general | solution.py:29
  74.2 7.6 %fusion.2 = f32[512,768]{1,0:T(8,128)S(1)} fusion(f32[1,768,768]{2,1,0:T(8,128)S(1)} %copy-done.3, f32[768,512]{1,0:T(8,128)S(1)} %copy-done.7, f32[768,512]{1,0:T(8,128)S(1)} %fusion.6, f32[768,512]{1,0:T(8,128)S(1)} %copy-done.8, f32[768,512]{1,0:T(8,128)S(1)} %fusion.10), kind=kOutput, calls=%fused_computation.2 | convolution fusion | flops 3625058304 | bytes 10223616 | tf_op jit(solution)/shard_map/...kl,...lr->...kr/dot_general | solution.py:29
  88.4 5.4 %collective-permute-done.9 = f32[128,512]{0,1:T(8,128)S(1)} collective-permute-done((f32[128,512]{0,1:T(8,128)S(1)}, f32[128,512]{0,1:T(8,128)S(1)}, u32[]{:S(2)}, u32[]{:S(2)}) %collective-permute-start.9) | collective-permute-done | bytes 262176 | tf_op jit(solution)/shard_map/ppermute | solution.py:25
  96.7 105.8 %all-reduce.5.cloned.1.call-done = (f32[128,512]{1,0:T(8,128)}, f32[128,128]{0,1:T(8,128)}, f32[128,128]{0,1:T(8,128)}, f32[128,128]{1,0:T(8,128)}, f32[128,128]{0,1:T(8,128)}) async-done(((f32[128,512]{1,0:T(8,128)}, f32[128,128]{0,1:T(8,128)}, f32[128,128]{0,1:T(8,128)}, f32[128,128]{1,0:T(8,128)}, f32[128,128]{0,1:T(8,128)}), (f32[128,512]{1,0:T(8,128)}, f32[128,128]{0,1:T(8,128)}, f32[128,128]{0,1:T(8,128)}, ...) | async-done | bytes 524304 | tf_op jit(solution)/shard_map/psum | solution.py:108
  205.6 12.5 %cholesky.70 = f32[128,128]{1,0:T(8,128)S(1)} custom-call(f32[128,128]{1,0:T(8,128)} %fusion.47), custom_call_target="Cholesky" | custom-call | tf_op jit(solution)/shard_map/jit(cholesky)/cholesky | solution.py:37
  220.0 10.6 %custom-call.27 = f32[1,128,128]{1,2,0:T(8,128)S(1)} custom-call(f32[1,128,128]{2,1,0:T(8,128)} %fusion.29), custom_call_target="InvertDiagBlocksLowerTriangular" | custom-call | tf_op jit(solution)/shard_map/triangular_solve/custom-call.2 | solution.py:39
  238.0 3.0 copy.21
  241.1 37.6 %all-reduce.7.cloned.1.call-done = (f32[128,512]{0,1:T(8,128)}, f32[128,128]{0,1:T(8,128)}) async-done(((f32[128,512]{0,1:T(8,128)}, f32[128,128]{0,1:T(8,128)}), (f32[128,512]{0,1:T(8,128)}, f32[128,128]{0,1:T(8,128)})) %all-reduce.7.cloned.1.call-update) | async-done | bytes 327696 | tf_op jit(solution)/shard_map/psum | solution.py:110
  281.8 13.4 %cholesky.81 = f32[128,128]{1,0:T(8,128)} custom-call(f32[128,128]{1,0:T(8,128)} %fusion.35), custom_call_target="Cholesky" | custom-call | tf_op jit(solution)/shard_map/jit(cholesky)/cholesky | solution.py:37
  298.7 11.3 %custom-call.33 = f32[1,128,128]{1,2,0:T(8,128)} custom-call(f32[1,128,128]{2,1,0:T(8,128)} %fusion.30), custom_call_target="InvertDiagBlocksLowerTriangular" | custom-call | tf_op jit(solution)/shard_map/triangular_solve/custom-call.4 | solution.py:39
  322.5 8.1 %collective-permute-start.11 = (f32[768,512]{0,1:T(8,128)}, f32[768,512]{0,1:T(8,128)}, u32[]{:S(2)}, u32[]{:S(2)}) collective-permute-start(f32[768,512]{0,1:T(8,128)} %fusion.16), channel_id=1, source_target_pairs={{1,0},{2,1},{3,2},{4,3},{5,4},{6,5},{7,6},{8,7},{9,8},{10,9},{11,1... | collective-permute-start | bytes 4718600 | tf_op jit(solution)/shard_map/ppermute | solution.py:17
  330.6 3.0 copy.22
  333.6 3.0 copy.23
  336.6 5.6 %fusion.12 = f32[512,768]{1,0:T(8,128)S(1)} fusion(f32[768,512]{0,1:T(8,128)} %fusion.16, f32[1,768,768]{2,1,0:T(8,128)S(1)} %copy-done), kind=kOutput, calls=%fused_computation.12 | convolution fusion | flops 3623878656 | bytes 5505024 | tf_op jit(solution)/shard_map/...kl,...lr->...kr/dot_general | solution.py:29
  342.3 4.5 %collective-permute-done.10 = f32[768,512]{0,1:T(8,128)} collective-permute-done((f32[768,512]{0,1:T(8,128)}, f32[768,512]{0,1:T(8,128)}, u32[]{:S(2)}, u32[]{:S(2)}) %collective-permute-start.10) | collective-permute-done | bytes 1572896 | tf_op jit(solution)/shard_map/ppermute | solution.py:14
  346.8 5.5 %fusion.8 = f32[512,768]{1,0:T(8,128)S(1)} fusion(f32[768,512]{0,1:T(8,128)} %collective-permute-done.10, f32[1,768,768]{2,1,0:T(8,128)S(1)} %copy-done.6), kind=kOutput, calls=%fused_computation.8 | convolution fusion | flops 3623878656 | bytes 5505024 | tf_op jit(solution)/shard_map/...kl,...lr->...kr/dot_general | solution.py:29
  352.3 6.8 %bitcast_subtract_fusion = f32[768,512]{0,1:T(8,128)} fusion(f32[768,512]{0,1:T(8,128)S(1)} %copy-done.9, f32[512,768]{1,0:T(8,128)S(1)} %fusion.12, f32[512,768]{1,0:T(8,128)S(1)} %fusion.8, f32[768,512]{0,1:T(8,128)} %collective-permute-done.11, f32[1,768,768]{2,1,0:T(8,128)S(1)} %copy-done.5), kind=kOutput, calls=%fused_computation.16 | convolution fusion | flops 3625058304 | bytes 10223616 | tf_op jit(solution)/shard_map/...kl,...lr->...kr/dot_general | solution.py:29
  359.1 3.0 copy.24
  (130 shorter events, 56.2 us)
Async XLA Ops:
  7.2 17.0 %copy-start = (f32[1,768,768]{2,1,0:T(8,128)S(1)}, f32[1,768,768]{2,1,0:T(8,128)}, u32[]{:S(2)}) copy-start(f32[1,768,768]{2,1,0:T(8,128)} %param.22) | copy-start | bytes 7077892
  7.2 195.3 %all-reduce.5.cloned.1.call-start = ((), (), s32[]{:S(2)}) async-start(), calls=%async_computation | async-start | bytes 1048576 | tf_op jit(solution)/shard_map/psum | solution.py:108
  7.2 54.9 %collective-permute-start = (f32[768,512]{1,0:T(8,128)}, f32[768,512]{1,0:T(8,128)}, u32[]{:S(2)}, u32[]{:S(2)}) collective-permute-start(f32[768,512]{1,0:T(8,128)} %param.21), channel_id=1, source_target_pairs={{0,1},{1,2},{2,3},{3,4},{4,5},{5,6},{6,7},{7,8},{8,9},{9,10},{10,1... | collective-permute-start | bytes 4718600 | tf_op jit(solution)/shard_map/ppermute | solution.py:14
  9.3 59.0 %collective-permute-start.1 = (f32[768,512]{1,0:T(8,128)}, f32[768,512]{1,0:T(8,128)}, u32[]{:S(2)}, u32[]{:S(2)}) collective-permute-start(f32[768,512]{1,0:T(8,128)} %param.21), channel_id=1, source_target_pairs={{1,0},{2,1},{3,2},{4,3},{5,4},{6,5},{7,6},{8,7},{9,8},{10,9},{11,1... | collective-permute-start | bytes 4718600 | tf_op jit(solution)/shard_map/ppermute | solution.py:17
  18.2 12.4 %collective-permute-start.6 = (f32[128,128]{0,1:T(8,128)S(1)}, f32[128,128]{0,1:T(8,128)}, u32[]{:S(2)}, u32[]{:S(2)}) collective-permute-start(f32[128,128]{0,1:T(8,128)S(1)} %bitcast.190), channel_id=1, source_target_pairs={{0,1},{1,0},{2,3},{3,2},{4,5},{5,4},{6,7},{7,6},{8,9},{9,8},{10,11... | collective-permute-start | bytes 196616 | tf_op jit(solution)/shard_map/ppermute | solution.py:25
  23.6 8.0 %collective-permute-start.4 = (f32[128,128]{0,1:T(8,128)S(1)}, f32[128,128]{0,1:T(8,128)}, u32[]{:S(2)}, u32[]{:S(2)}) collective-permute-start(f32[128,128]{0,1:T(8,128)S(1)} %convolution_bitcast_fusion.3), channel_id=1, source_target_pairs={{0,1},{1,0},{2,3},{3,2},{4,5},{5,4},{6,7},{7,6},{8,9},{9,8},{10,11... | collective-permute-start | bytes 196616 | tf_op jit(solution)/shard_map/ppermute | solution.py:25
  24.0 10.5 %collective-permute-start.2 = (f32[128,128]{1,0:T(8,128)S(1)}, f32[128,128]{1,0:T(8,128)}, u32[]{:S(2)}, u32[]{:S(2)}) collective-permute-start(f32[128,128]{1,0:T(8,128)S(1)} %bitcast.193), channel_id=1, source_target_pairs={{0,1},{1,0},{2,3},{3,2},{4,5},{5,4},{6,7},{7,6},{8,9},{9,8},{10,11... | collective-permute-start | bytes 196616 | tf_op jit(solution)/shard_map/ppermute | solution.py:25
  31.5 4.9 %collective-permute-start.7 = (f32[128,128]{0,1:T(8,128)S(1)}, f32[128,128]{0,1:T(8,128)S(1)}, u32[]{:S(2)}, u32[]{:S(2)}) collective-permute-start(f32[128,128]{0,1:T(8,128)S(1)} %bitcast_add_fusion.3), channel_id=1, source_target_pairs={{0,2},{1,3},{2,0},{3,1},{4,6},{5,7},{6,4},{7,5},{8,10},{9,11},{10,... | collective-permute-start | bytes 196616 | tf_op jit(solution)/shard_map/ppermute | solution.py:25
  32.4 4.9 %collective-permute-start.5 = (f32[128,128]{0,1:T(8,128)S(1)}, f32[128,128]{0,1:T(8,128)S(1)}, u32[]{:S(2)}, u32[]{:S(2)}) collective-permute-start(f32[128,128]{0,1:T(8,128)S(1)} %add.94), channel_id=1, source_target_pairs={{0,2},{1,3},{2,0},{3,1},{4,6},{5,7},{6,4},{7,5},{8,10},{9,11},{10,... | collective-permute-start | bytes 196616 | tf_op jit(solution)/shard_map/ppermute | solution.py:25
  35.4 48.6 %collective-permute-start.3 = (f32[128,128]{1,0:T(8,128)S(1)}, f32[128,128]{1,0:T(8,128)S(1)}, u32[]{:S(2)}, u32[]{:S(2)}) collective-permute-start(f32[128,128]{1,0:T(8,128)S(1)} %bitcast_add_fusion.4), channel_id=1, source_target_pairs={{0,2},{1,3},{2,0},{3,1},{4,6},{5,7},{6,4},{7,5},{8,10},{9,11},{10,... | collective-permute-start | bytes 196616 | tf_op jit(solution)/shard_map/ppermute | solution.py:25
  37.3 57.4 %copy-start.15 = (f32[128,128]{0,1:T(8,128)}, f32[128,128]{0,1:T(8,128)S(1)}, u32[]{:S(2)}) copy-start(f32[128,128]{0,1:T(8,128)S(1)} %get-tuple-element.17) | copy-start | bytes 196612
  62.1 6.2 %copy-start.4 = (f32[1,768,768]{2,1,0:T(8,128)S(1)}, f32[1,768,768]{2,1,0:T(8,128)}, u32[]{:S(2)}) copy-start(f32[1,768,768]{2,1,0:T(8,128)} %param.24) | copy-start | bytes 7077892
  68.2 6.0 %copy-start.3 = (f32[1,768,768]{2,1,0:T(8,128)S(1)}, f32[1,768,768]{2,1,0:T(8,128)}, u32[]{:S(2)}) copy-start(f32[1,768,768]{2,1,0:T(8,128)} %param.25) | copy-start | bytes 7077892
  68.2 6.0 %copy-start.7 = (f32[768,512]{1,0:T(8,128)S(1)}, f32[768,512]{1,0:T(8,128)}, u32[]{:S(2)}) copy-start(f32[768,512]{1,0:T(8,128)} %param.20) | copy-start | bytes 4718596
  83.6 1.6 collective-permute-start.8
  85.3 8.6 %collective-permute-start.9 = (f32[128,512]{0,1:T(8,128)S(1)}, f32[128,512]{0,1:T(8,128)S(1)}, u32[]{:S(2)}, u32[]{:S(2)}) collective-permute-start(f32[128,512]{0,1:T(8,128)S(1)} %add.101), channel_id=1, source_target_pairs={{0,2},{1,3},{2,0},{3,1},{4,6},{5,7},{6,4},{7,5},{8,10},{9,11},{10,... | collective-permute-start | bytes 786440 | tf_op jit(solution)/shard_map/ppermute | solution.py:25
  96.4 182.2 %all-reduce.7.cloned.1.call-start = ((), (), s32[]{:S(2)}) async-start(), calls=%async_computation.1 | async-start | bytes 655360 | tf_op jit(solution)/shard_map/psum | solution.py:110
  202.5 32.6 %copy-start.13 = (f32[128,512]{1,0:T(8,128)S(1)}, f32[128,512]{1,0:T(8,128)}, u32[]{:S(2)}) copy-start(f32[128,512]{1,0:T(8,128)} %get-tuple-element.8) | copy-start | bytes 786436
  202.5 32.6 %copy-start.14 = (f32[128,128]{0,1:T(8,128)S(1)}, f32[128,128]{0,1:T(8,128)}, u32[]{:S(2)}) copy-start(f32[128,128]{0,1:T(8,128)} %get-tuple-element.10) | copy-start | bytes 196612
  320.5 26.3 %collective-permute-start.10 = (f32[768,512]{0,1:T(8,128)}, f32[768,512]{0,1:T(8,128)}, u32[]{:S(2)}, u32[]{:S(2)}) collective-permute-start(f32[768,512]{0,1:T(8,128)} %fusion.16), channel_id=1, source_target_pairs={{0,1},{1,2},{2,3},{3,4},{4,5},{5,6},{6,7},{7,8},{8,9},{9,10},{10,1... | collective-permute-start | bytes 4718600 | tf_op jit(solution)/shard_map/ppermute | solution.py:14
  322.5 29.8 %collective-permute-start.11 = (f32[768,512]{0,1:T(8,128)}, f32[768,512]{0,1:T(8,128)}, u32[]{:S(2)}, u32[]{:S(2)}) collective-permute-start(f32[768,512]{0,1:T(8,128)} %fusion.16), channel_id=1, source_target_pairs={{1,0},{2,1},{3,2},{4,3},{5,4},{6,5},{7,6},{8,7},{9,8},{10,9},{11,1... | collective-permute-start | bytes 4718600 | tf_op jit(solution)/shard_map/ppermute | solution.py:17
  336.6 10.2 %copy-start.6 = (f32[1,768,768]{2,1,0:T(8,128)S(1)}, f32[1,768,768]{2,1,0:T(8,128)}, u32[]{:S(2)}) copy-start(f32[1,768,768]{2,1,0:T(8,128)} %param.23) | copy-start | bytes 7077892
  342.2 10.0 %copy-start.5 = (f32[1,768,768]{2,1,0:T(8,128)S(1)}, f32[1,768,768]{2,1,0:T(8,128)}, u32[]{:S(2)}) copy-start(f32[1,768,768]{2,1,0:T(8,128)} %param.24) | copy-start | bytes 7077892
  342.2 10.0 %copy-start.9 = (f32[768,512]{0,1:T(8,128)S(1)}, f32[768,512]{0,1:T(8,128)}, u32[]{:S(2)}) copy-start(f32[768,512]{0,1:T(8,128)} %copy.22) | copy-start | bytes 4718596
  (12 other events, 46.8 us)
Sparse Core Ops, SparseCore 0:
  96.6 105.8 all-reduce.4
  238.2 40.4 all-reduce.6
where the time goes:
time: 377 us; the launch traced here: 369 us
  waiting for transfers between devices  156 us (41%)
  other arithmetic  84.2 us (22%)
  matrix products  71.5 us (19%)
  starting transfers between devices  25.4 us (7%)
  local copies, waits for them, and re-layouts  17.1 us (5%)
  between operations  15.2 us (4%)
    psum x1, waiting for transfers between devices, body(): group_rhs = lax.psum(leader * across(block_mid, block_red), 'leaf')  106 us
    dot_general x21, matrix products, product(): return jnp.einsum('...kl,...lr->...kr', left, right, precision=highest)  55.6 us
    another operation x9, other arithmetic, definite_solve(): factor = jnp.linalg.cholesky(matrix)  41.3 us
    psum x1, waiting for transfers between devices, body(): root_rhs = lax.psum(across(group_top, group_red), 'grp')  37.6 us
    another operation x6, other arithmetic, definite_solve(): lax.linalg.triangular_solve(factor, halfway, left_side=True, lower=True,...  35.7 us
    ppermute x2, starting transfers between devices, with_halo(): lax.ppermute(lax.slice_in_dim(block, 0, width, axis=dim), axis, backward)  16 us
    unnamed x51, local copies, waits for them, and re-layouts  13.8 us
    ppermute x8, waiting for transfers between devices, from_partner(): return lax.ppermute(value, axis, pairs)  8.03 us
  transfers between devices with their start and end apart: 14, of which 7 were waited for; matrix products, arithmetic and copies ran while one was open for 22% of the time, Pallas kernels for 0%

commit v1 on v0

v1 whole, which is shorter than its diff:
```python
import jax
import jax.numpy as jnp
from jax import lax
from jax.experimental import pallas as pl
from jax.experimental.pallas import tpu as pltpu
from jax.sharding import PartitionSpec as P

MESH = pl.DeviceIdType.MESH
F32 = jnp.float32
BF16 = jnp.bfloat16
LEAF, RANK, RHS = 768, 128, 512
HALF = RHS // 2


def dot(left, right, over=(1, 0)):
    return lax.dot_general(
        left,
        right,
        (((over[0],), (over[1],)), ((), ())),
        precision=lax.Precision.HIGHEST,
        preferred_element_type=F32,
    )


def split(value):
    high = value.astype(BF16)
    return high, (value - high.astype(F32)).astype(BF16)


def plain(left, right, over=(1, 0)):
    return lax.dot_general(
        left, right, (((over[0],), (over[1],)), ((), ())), preferred_element_type=F32
    )


def stacked(pair_ref, value):
    count = pair_ref.shape[0] // 2
    high, low = split(value)
    both = plain(pair_ref[...], high)
    return both[:count] + both[count:] + plain(pair_ref[:count], low)


def spd_inverse(a):
    lane = lax.broadcasted_iota(jnp.int32, (8, 128), 1)
    sub = lax.broadcasted_iota(jnp.int32, (8, 128), 0)
    head = lane < 8
    unit = jnp.where(lane == sub, -1.0, 0.0)

    def step(_, rows):
        p = rows[0]
        sc = {}
        for i in range(8):
            for k in range(i, 8):
                sc[i, k] = jnp.broadcast_to(p[i:i + 1, k:k + 1], (8, 128))
        get = lambda i, k: sc[min(i, k), max(i, k)]
        for q in range(0, 8, 2):
            aa, bb, cc = sc[q, q], sc[q, q + 1], sc[q + 1, q + 1]
            inv = 1.0 / (aa * cc - bb * bb)
            ia, ib, ic = cc * inv, -bb * inv, aa * inv
            others = [i for i in range(8) if i not in (q, q + 1)]
            p0 = {i: get(i, q) for i in others}
            p1 = {i: get(i, q + 1) for i in others}
            q0 = {i: ia * p0[i] + ib * p1[i] for i in others}
            q1 = {i: ib * p0[i] + ic * p1[i] for i in others}
            for i in others:
                for k in others:
                    if i <= k:
                        sc[i, k] = sc[i, k] - (p0[i] * q0[k] + p1[i] * q1[k])
            for i in others:
                sc[min(i, q), max(i, q)] = q0[i]
                sc[min(i, q + 1), max(i, q + 1)] = q1[i]
            sc[q, q], sc[q, q + 1], sc[q + 1, q + 1] = -ia, -ib, -ic
        pm = jnp.where(head, unit, p)
        pb = [jnp.broadcast_to(pm[m:m + 1, :], (8, 128)) for m in range(8)]
        nq = []
        for k in range(8):
            t = get(k, 0) * pb[0]
            for m in range(1, 8):
                t = t + get(k, m) * pb[m]
            nq.append(t)
        out = []
        for i in range(1, 16):
            r = rows[i]
            t = jnp.where(head, 0.0, r)
            for k in range(8):
                t = t + jnp.broadcast_to(r[:, k:k + 1], (8, 128)) * nq[k]
            out.append(pltpu.roll(t, 120, 1))
        t = nq[7]
        for k in range(7):
            t = jnp.where(sub == k, nq[k], t)
        out.append(pltpu.roll(-t, 120, 1))
        return tuple(out)

    rows = tuple(a[8 * i:8 * i + 8, :] for i in range(16))
    rows = lax.fori_loop(0, 16, step, rows)
    return -jnp.concatenate(rows, 0)

def tree_kernel(
    right_h,
    guess_h,
    diag_h,
    lower_h,
    upper_h,
    inverse_h,
    basis_h,
    trans_h,
    mid_h,
    top_h,
    coup_h,
    base_o,
    left_o,
    out_o,
    cross_o,
    node_o,
    wide,
    pairs,
    right,
    guess,
    resid,
    sol,
    base,
    halo,
    halo2,
    basis,
    trans,
    expand,
    expand_halo,
    project,
    share,
    proj,
    e1s,
    e1p,
    three,
    node_m,
    xs_out,
    xs_in,
    zs_out,
    zs_in,
    group_m,
    q_out,
    xq_in,
    zq_out,
    zq_in,
    gp_out,
    root_out,
    root_in,
    reduced,
    r1_in,
    v_out,
    r2_in,
    u_out,
    r3_in,
    gout,
    block_own,
    block_out,
    block_halo,
    load_sem,
    store_sem,
    send_sem,
    recv_sem,
):
    y = lax.axis_index("grp")
    l = lax.axis_index("leaf")
    j = l % 4
    node = l // 4
    first = l - j
    index = y * 32 + l

    def at(place):
        place = place % 128
        return (place // 32, place % 32)

    nxt, prv = at(index + 1), at(index + 127)
    spots = [(j + d) % 4 for d in (1, 2, 3)]
    mates = [(y, first + spot) for spot in spots]
    cross = [(y, (l + 8 * d) % 32) for d in (1, 2, 3)]
    across_z = (y, l + 4 - 8 * (node % 2))
    peers = [(y, (l + 4 * d) % 32) for d in range(1, 8)]
    peer_spots = [(node + d) % 8 for d in range(1, 8)]
    ring = [((y + d) % 4, l) for d in (1, 2, 3)]

    counter = [0]
    sent = []

    def remote(src, dst, device, start=True):
        k = counter[0]
        counter[0] += 1
        copy = pltpu.make_async_remote_copy(
            src_ref=src,
            dst_ref=dst,
            send_sem=send_sem.at[k],
            recv_sem=recv_sem.at[k],
            device_id=device,
            device_id_type=MESH,
        )
        if start:
            copy.start()
        sent.append(copy)
        return copy

    def arrived(copies):
        for copy in copies:
            copy.wait_recv()

    local = []

    def load(src, dst):
        copy = pltpu.make_async_copy(src, dst, load_sem.at[len(local)])
        copy.start()
        local.append(copy)
        return copy

    load_share = [
        load(coup_h, share.at[pl.ds(0, 3)]),
        load(mid_h, share.at[3]),
        load(top_h, share.at[4]),
    ]
    load_inverse = load(inverse_h, wide.at[3])
    load_basis = load(basis_h, basis)
    load_trans = load(trans_h, trans)
    load_guess = load(guess_h, guess)
    load_diag = load(diag_h, wide.at[0])
    load_right = load(right_h, right)
    load_lower = load(lower_h, wide.at[1])
    load_upper = load(upper_h, wide.at[2])

    barrier = pltpu.get_barrier_semaphore()
    for device in [nxt, prv] + mates + peers + ring:
        pl.semaphore_signal(barrier, inc=1, device_id=device, device_id_type=MESH)

    @pl.when(j == 0)
    def _():
        for k in range(4):
            pl.semaphore_signal(
                barrier, inc=1, device_id=at(index + 124 + k), device_id_type=MESH
            )

    @pl.when(j == 3)
    def _():
        for k in range(4):
            pl.semaphore_signal(
                barrier, inc=1, device_id=at(index + 1 + k), device_id_type=MESH
            )

    pl.semaphore_wait(barrier, 17)

    def cols(c):
        return pl.ds(c * HALF, HALF)

    halo_in = []
    for c in range(2):
        halo_in.append(
            [
                remote(guess_h.at[:, cols(c)], halo.at[0, :, cols(c)], nxt),
                remote(guess_h.at[:, cols(c)], halo.at[1, :, cols(c)], prv),
            ]
        )

    for copy in load_share:
        copy.wait()
    e1_static = [
        remote(share.at[:, pl.ds(spots[d] * 32, 32)], e1s.at[d], mates[d]) for d in range(3)
    ]

    def divide(m, scale=None):
        value = wide[m]
        if scale is not None:
            value = value * scale
        high, low = split(value)
        pairs[m, pl.ds(0, LEAF)] = high
        pairs[m, pl.ds(LEAF, LEAF)] = low

    load_inverse.wait()
    load_basis.wait()
    load_trans.wait()
    divide(3)
    basis_t = basis[...].T
    trans_t = trans[...].T
    weighted = dot(wide[3], basis[...])
    expand[...] = dot(weighted, trans[...])
    proj[...] = dot(trans_t, dot(dot(basis_t, weighted), trans[...]))
    e1_proj = [
        remote(proj.at[pl.ds(spots[d] * 32, 32)], e1p.at[d], mates[d]) for d in range(3)
    ]
    expand_in = [
        remote(expand, expand_halo.at[0], nxt),
        remote(expand, expand_halo.at[1], prv),
    ]
    high, low = split(dot(trans_t, basis_t))
    project[pl.ds(0, RANK)] = high
    project[pl.ds(RANK, RANK)] = low

    load_guess.wait()
    load_diag.wait()
    load_right.wait()
    divide(0)

    def own(c, carry):
        here = pl.ds(pl.multiple_of(c * HALF, HALF), HALF)
        resid[:, here] = right[:, here] - stacked(pairs.at[0], guess[:, here])
        return carry

    lax.fori_loop(0, 2, own, 0)

    rows = pl.ds(pl.multiple_of(j * 32, 32), 32)
    arrived(e1_static)
    sums = share[:, rows] + e1s[0] + e1s[1] + e1s[2]
    xs_out[0:2] = sums[1:3]
    xs_out[2] = sums[4]
    xs_copies = [remote(xs_out, xs_in.at[d], cross[d]) for d in range(3)]
    arrived(e1_proj)
    three[0] = proj[rows] + e1p[0] + e1p[1] + e1p[2]
    three[1] = sums[0]
    three[2] = sums[3]
    node_m[:, rows] = three[...]
    e2 = [remote(three, node_m.at[:, rows], mates[d]) for d in range(3)]

    load_lower.wait()
    load_upper.wait()
    divide(1, jnp.where(index == 0, 0.0, 1.0))
    divide(2, jnp.where(index == 127, 0.0, 1.0))

    arrived(xs_copies)
    zs_out[...] = xs_out[...] + xs_in[0] + xs_in[1] + xs_in[2]
    zs_copy = remote(zs_out, zs_in, across_z)

    arrived(e2)
    p_proj, p_coup, p_mid = node_m[0], node_m[1], node_m[2]
    p_inv = spd_inverse(p_proj + p_coup)
    fm = dot(dot(p_inv, p_coup), p_mid)
    mf = fm.T
    q_node = dot(mf, dot(p_proj, p_mid))
    q_out[...] = q_node
    xq_copies = [remote(q_out.at[rows], xq_in.at[d], cross[d]) for d in range(3)]

    arrived([zs_copy])
    gstat = zs_out[...] + zs_in[...]
    xs_sum = gstat
    group_m[pl.ds(0, 3), rows] = xs_sum
    e4_static = [
        remote(group_m.at[pl.ds(0, 3), rows], group_m.at[pl.ds(0, 3), rows], mates[d])
        for d in range(3)
    ]

    def leaf_chunk(c):
        here = cols(c)
        arrived(halo_in[c])

        def side(k, carry):
            resid[:, here] = resid[:, here] - stacked(pairs.at[k + 1], halo[k, :, here])
            return carry

        lax.fori_loop(0, 2, side, 0)
        sol[:, here] = stacked(pairs.at[3], resid[:, here])
        return [
            remote(sol.at[:, here], halo2.at[0, :, here], nxt),
            remote(sol.at[:, here], halo2.at[1, :, here], prv),
        ]

    def reduce_chunk(c):
        here = cols(c)
        reduced[here, :] = stacked(project, sol[:, here]).T
        base[:, here] = guess[:, here] + sol[:, here]

    halo2_in = [leaf_chunk(0)]

    arrived(xq_copies)
    zq_out[...] = q_out[rows] + xq_in[0] + xq_in[1] + xq_in[2]
    zq_copy = remote(zq_out, zq_in, across_z)
    reduce_chunk(0)

    arrived([zq_copy])
    gp_out[...] = zq_out[...] + zq_in[...]
    group_m[3, rows] = gp_out[...]
    e4 = [remote(gp_out, group_m.at[3, rows], mates[d]) for d in range(3)]

    halo2_in.append(leaf_chunk(1))
    reduce_chunk(1)
    r1_copies = [
        remote(reduced.at[pl.ds(spots[d] * 128, 128)], r1_in.at[d], mates[d]) for d in range(3)
    ]

    arrived(e4_static)
    arrived(e4)
    g_coup, r_coup, g_top, g_proj = group_m[0], group_m[1], group_m[2], group_m[3]
    g_inv = spd_inverse(g_proj + g_coup)
    gf_t = dot(g_inv, g_coup)
    ft = dot(gf_t, g_top)
    ft_t = ft.T
    root_out[...] = r_coup + dot(ft_t, dot(g_proj, g_top))
    root_copies = [remote(root_out, root_in.at[d], ring[d]) for d in range(3)]

    arrived(r1_copies)
    wide_rows = pl.ds(pl.multiple_of(j * 128, 128), 128)
    block_rhs = reduced[wide_rows] + r1_in[0] + r1_in[1] + r1_in[2]
    v_out[...] = dot(block_rhs, fm)
    r2_copies = [
        remote(v_out.at[pl.ds(peer_spots[d] * 16, 16)], r2_in.at[d], peers[d]) for d in range(7)
    ]
    block_part = dot(block_rhs, p_inv)

    def again(c, carry):
        here = pl.ds(pl.multiple_of(c * HALF, HALF), HALF)
        resid[:, here] = resid[:, here] - stacked(pairs.at[0], sol[:, here])
        return carry

    lax.fori_loop(0, 2, again, 0)
    arrived(expand_in)
    cross_o[:, pl.ds(0, RANK)] = stacked(pairs.at[0], expand[...])
    for k in range(2):
        cross_o[:, pl.ds((k + 1) * RANK, RANK)] = stacked(pairs.at[k + 1], expand_halo[k])
    out_o[...] = expand[...]

    arrived(r2_copies)
    few_rows = pl.ds(pl.multiple_of(node * 16, 16), 16)
    group_rhs = v_out[few_rows]
    for d in range(7):
        group_rhs = group_rhs + r2_in[d]
    u_out[...] = dot(group_rhs, ft)
    r3_copies = [remote(u_out, r3_in.at[d], ring[d]) for d in range(3)]
    group_part = dot(group_rhs, g_inv)

    arrived(root_copies)
    r_inv = spd_inverse(root_out[...] + root_in[0] + root_in[1] + root_in[2])
    down = dot(r_inv, ft_t)

    arrived(r3_copies)
    root_rhs = u_out[...] + r3_in[0] + r3_in[1] + r3_in[2]
    gout[few_rows] = group_part + dot(root_rhs, down)
    r4_copies = [remote(gout.at[few_rows], gout.at[few_rows], peers[d]) for d in range(7)]

    for c in range(2):
        here = cols(c)
        arrived(halo2_in[c])

        def side2(k, carry):
            resid[:, here] = resid[:, here] - stacked(pairs.at[k + 1], halo2[k, :, here])
            return carry

        lax.fori_loop(0, 2, side2, 0)

    stores = [
        pltpu.make_async_copy(base, base_o, store_sem.at[0]),
        pltpu.make_async_copy(resid, left_o, store_sem.at[1]),
    ]
    for copy in stores:
        copy.start()

    arrived(r4_copies)
    block_own[...] = block_part + dot(gout[...], mf)
    block_out[wide_rows] = block_own[...]
    r5_copies = [remote(block_own, block_out.at[wide_rows], mates[d]) for d in range(3)]
    k5 = counter[0]
    ahead = [at(index - j + 4), at(index - j + 127)]
    extra = [
        pltpu.make_async_remote_copy(
            src_ref=block_own,
            dst_ref=block_halo.at[wide_rows],
            send_sem=send_sem.at[k5 + way],
            recv_sem=recv_sem.at[k5 + 2 + j],
            device_id=ahead[way],
            device_id_type=MESH,
        )
        for way in range(2)
    ]
    for copy in extra:
        copy.start()

    arrived(r5_copies)
    for k in range(3):
        node_o[:, pl.ds(k * RANK, RANK)] = block_out[...]

    def from_halo(k):
        for spot in range(4):
            pltpu.make_async_remote_copy(
                src_ref=block_own,
                dst_ref=block_halo.at[pl.ds(spot * 128, 128)],
                send_sem=send_sem.at[k5],
                recv_sem=recv_sem.at[k5 + 2 + spot],
                device_id=ahead[0],
                device_id_type=MESH,
            ).wait_recv()
        node_o[:, pl.ds(k * RANK, RANK)] = block_halo[...]

    @pl.when(j == 0)
    def _():
        from_halo(1)

    @pl.when(j == 3)
    def _():
        from_halo(2)

    for copy in sent:
        copy.wait_send()
    for copy in extra:
        copy.wait_send()
    for copy in stores:
        copy.wait()


def last_kernel(base_ref, left_ref, out_ref, cross_ref, node_ref, guess_ref, resid_ref):
    def three(left, right):
        left_high, left_low = split(left)
        right_high, right_low = split(right)
        over = (1, 1)
        return (
            plain(left_high, right_high, over)
            + plain(left_low, right_high, over)
            + plain(left_high, right_low, over)
        )

    node = node_ref[...]
    guess_ref[...] = base_ref[...] - three(out_ref[...], node[:, :RANK])
    resid_ref[...] = left_ref[...] + three(cross_ref[...], node)


def tree(*args):
    any_spec = pl.BlockSpec(memory_space=pl.ANY)
    vmem = pl.BlockSpec(memory_space=pltpu.VMEM)

    def buf(*shape, dtype=F32):
        return pltpu.VMEM(shape, dtype)

    scratch = [
        buf(4, LEAF, LEAF),
        buf(4, 2 * LEAF, LEAF, dtype=BF16),
        buf(LEAF, RHS),
        buf(LEAF, RHS),
        buf(LEAF, RHS),
        buf(LEAF, RHS),
        buf(LEAF, RHS),
        buf(2, LEAF, RHS),
        buf(2, LEAF, RHS),
        buf(LEAF, RANK),
        buf(RANK, RANK),
        buf(LEAF, RANK),
        buf(2, LEAF, RANK),
        buf(2 * RANK, LEAF, dtype=BF16),
        buf(5, RANK, RANK),
        buf(RANK, RANK),
        buf(3, 5, 32, RANK),
        buf(3, 32, RANK),
        buf(3, 32, RANK),
        buf(3, RANK, RANK),
        buf(3, 32, RANK),
        buf(3, 3, 32, RANK),
        buf(3, 32, RANK),
        buf(3, 32, RANK),
        buf(4, RANK, RANK),
        buf(RANK, RANK),
        buf(3, 32, RANK),
        buf(32, RANK),
        buf(32, RANK),
        buf(32, RANK),
        buf(RANK, RANK),
        buf(3, RANK, RANK),
        buf(RHS, RANK),
        buf(3, RANK, RANK),
        buf(RANK, RANK),
        buf(7, 16, RANK),
        buf(16, RANK),
        buf(3, 16, RANK),
        buf(RANK, RANK),
        buf(RANK, RANK),
        buf(RHS, RANK),
        buf(RHS, RANK),
        pltpu.SemaphoreType.DMA((11,)),
        pltpu.SemaphoreType.DMA((2,)),
        pltpu.SemaphoreType.DMA((72,)),
        pltpu.SemaphoreType.DMA((72,)),
    ]
    base, left, out, cross, node = pl.pallas_call(
        tree_kernel,
        out_shape=[
            jax.ShapeDtypeStruct((LEAF, RHS), F32),
            jax.ShapeDtypeStruct((LEAF, RHS), F32),
            jax.ShapeDtypeStruct((LEAF, RANK), F32),
            jax.ShapeDtypeStruct((LEAF, 3 * RANK), F32),
            jax.ShapeDtypeStruct((RHS, 3 * RANK), F32),
        ],
        in_specs=[any_spec] * 11,
        out_specs=[any_spec, any_spec, vmem, vmem, vmem],
        scratch_shapes=scratch,
        compiler_params=pltpu.CompilerParams(
            collective_id=0, has_side_effects=True, vmem_limit_bytes=56 * 2**20
        ),
    )(*args)
    block = 256
    return pl.pallas_call(
        last_kernel,
        grid=(LEAF // block,),
        in_specs=[
            pl.BlockSpec((block, RHS), lambda i: (i, 0)),
            pl.BlockSpec((block, RHS), lambda i: (i, 0)),
            pl.BlockSpec((block, RANK), lambda i: (i, 0)),
            pl.BlockSpec((block, 3 * RANK), lambda i: (i, 0)),
            pl.BlockSpec((RHS, 3 * RANK), lambda i: (0, 0)),
        ],
        out_specs=[
            pl.BlockSpec((block, RHS), lambda i: (i, 0)),
            pl.BlockSpec((block, RHS), lambda i: (i, 0)),
        ],
        out_shape=[jax.ShapeDtypeStruct((LEAF, RHS), F32)] * 2,
    )(base, left, out, cross, node)


def body(
    right_side,
    guess,
    near_diag,
    near_lower,
    near_upper,
    leaf_inverse,
    leaf_basis,
    leaf_transfer,
    mid_share,
    top_share,
    coupling_share,
):
    new_guess, new_residual = tree(
        right_side,
        guess,
        near_diag[0],
        near_lower[0],
        near_upper[0],
        leaf_inverse[0],
        leaf_basis[0],
        leaf_transfer[0],
        mid_share[0],
        top_share[0],
        coupling_share[0],
    )
    return (new_guess, new_residual)


def solution(mesh):
    field = P(("grp", "leaf"), None)
    block = P(("grp", "leaf"), None, None)
    shares = P(("grp", "leaf"), None, None, None)
    in_specs = (field, field) + (block,) * 8 + (shares,)
    return jax.shard_map(
        body, mesh=mesh, in_specs=in_specs, out_specs=(field, field), check_vma=False
    )
```

time: 377 us -> 113 us (0.30)
  the two profiles are of different devices: /device:TPU:16 before, /device:TPU:33 now
where the time goes in v1:
time: 113 us; the launch traced here: 112 us
  Pallas kernels  111 us (98%)
    pallas_call x1, Pallas kernels, tree(): pl.pallas_call(tree_kernel, out_shape=[jax.ShapeDtypeStruct((LEAF, RHS),...  105 us
    pallas_call x1, Pallas kernels, tree(): pl.pallas_call(last_kernel, grid=(LEAF // block,), in_specs=[pl.BlockSpec...  6.14 us

profile of v1, /device:TPU:33, one launch (start us, length us, event | category | flops | bytes accessed | tf_op | source)
XLA Modules:
  0.0 112.1 jit_solution(12505189033229105746)
XLA Ops:
  0.6 105.3 %shard_map.122 = (f32[768,512]{1,0:T(8,128)}, f32[768,512]{1,0:T(8,128)}, f32[768,128]{1,0:T(8,128)}, f32[768,384]{1,0:T(8,128)}, f32[512,384]{1,0:T(8,128)}) custom-call(f32[768,512]{1,0:T(8,128)} %right_h.1, f32[768,512]{1,0:T(8,128)} %guess_h.1, f32[768,768]{1,0:T(8,128)} %bitcast.9, f32[768,768]{1,0:T(8,128)} %bitcast.10, f32[768,768]{1,0:T(8,128)} %bitcast.11, ...), custom_call_target="tpu_custom_call" | custom-call | tf_op jit(solution)/shard_map/pallas_call | solution.py:572
  105.9 6.1 %shard_map.123 = (f32[768,512]{1,0:T(8,128)}, f32[768,512]{1,0:T(8,128)}) custom-call(f32[768,512]{1,0:T(8,128)} %get-tuple-element.7.base_ref, f32[768,512]{1,0:T(8,128)} %get-tuple-element.8.left_ref, f32[768,128]{1,0:T(8,128)} %get-tuple-element.9.out_ref, f32[768,384]{1,0:T(8,128)} %get-tuple-element.10.cross_ref, f32[512,384]{1,0:T(8,128)} %get-tuple-element.11.node_ref), custom_call_target="tpu_custom_call" | custom-call | tf_op jit(solution)/shard_map/pallas_call | solution.py:589

commit v2 on v1

v2 whole, which is shorter than its diff:
```python
import jax
import jax.numpy as jnp
from jax import lax
from jax.experimental import pallas as pl
from jax.experimental.pallas import tpu as pltpu
from jax.sharding import PartitionSpec as P

MESH = pl.DeviceIdType.MESH
F32 = jnp.float32
BF16 = jnp.bfloat16
LEAF, RANK, RHS = 768, 128, 512
HALF = RHS // 2


def dot(left, right, over=(1, 0)):
    return lax.dot_general(
        left,
        right,
        (((over[0],), (over[1],)), ((), ())),
        precision=lax.Precision.HIGHEST,
        preferred_element_type=F32,
    )


def split(value):
    high = value.astype(BF16)
    return high, (value - high.astype(F32)).astype(BF16)


def plain(left, right, over=(1, 0)):
    return lax.dot_general(
        left, right, (((over[0],), (over[1],)), ((), ())), preferred_element_type=F32
    )


def stacked(pair_ref, value):
    count = pair_ref.shape[0] // 2
    high, low = split(value)
    both = plain(pair_ref[...], high)
    return both[:count] + both[count:] + plain(pair_ref[:count], low)


def spd_inverse(matrix):
    lane = lax.broadcasted_iota(jnp.int32, (8, 128), 1)
    sub = lax.broadcasted_iota(jnp.int32, (8, 128), 0)

    def total(t):
        return ((t[0] + t[1]) + (t[2] + t[3])) + ((t[4] + t[5]) + (t[6] + t[7]))

    def panel(rows, s):
        at = 8 * s
        head = (lane >= at) & (lane < at + 8)
        p = rows[s]
        sc = {}
        for k in range(8):
            col = jnp.broadcast_to(p[:, at + k : at + k + 1], (8, 128))
            for i in range(k + 1):
                sc[i, k] = jnp.broadcast_to(col[i : i + 1, :], (8, 128))

        def get(i, k):
            return sc[min(i, k), max(i, k)]

        for q in range(0, 8, 2):
            aa, bb, cc = sc[q, q], sc[q, q + 1], sc[q + 1, q + 1]
            det = aa * cc - bb * bb
            inv = pl.reciprocal(det, approx=True)
            inv = inv * (2.0 - det * inv)
            inv = inv * (2.0 - det * inv)
            ia, ib, ic = cc * inv, -bb * inv, aa * inv
            others = [i for i in range(8) if i not in (q, q + 1)]
            p0 = {i: get(i, q) for i in others}
            p1 = {i: get(i, q + 1) for i in others}
            q0 = {i: ia * p0[i] + ib * p1[i] for i in others}
            q1 = {i: ib * p0[i] + ic * p1[i] for i in others}
            for i in others:
                for k in others:
                    if i <= k:
                        sc[i, k] = sc[i, k] - (p0[i] * q0[k] + p1[i] * q1[k])
            for i in others:
                sc[min(i, q), max(i, q)] = q0[i]
                sc[min(i, q + 1), max(i, q + 1)] = q1[i]
            sc[q, q], sc[q, q + 1], sc[q + 1, q + 1] = -ia, -ib, -ic
        pm = jnp.where(head, jnp.where(lane == sub + at, -1.0, 0.0), p)
        pb = [jnp.broadcast_to(pm[m : m + 1, :], (8, 128)) for m in range(8)]
        nq = [total([get(k, m) * pb[m] for m in range(8)]) for k in range(8)]
        out = list(rows)
        for i in [(s + 1 + i) % 16 for i in range(15)]:
            r = rows[i]
            terms = [
                jnp.broadcast_to(r[:, at + k : at + k + 1], (8, 128)) * nq[k] for k in range(8)
            ]
            out[i] = jnp.where(head, 0.0, r) + total(terms)
        t = nq[7]
        for k in range(7):
            t = jnp.where(sub == k, nq[k], t)
        out[s] = -t
        return out

    def step(_, rows):
        rows = list(rows)
        for s in range(4):
            rows = panel(rows, s)
        rows = [pltpu.roll(r, 96, 1) for r in rows]
        return tuple(rows[4:] + rows[:4])

    rows = tuple(matrix[8 * i : 8 * i + 8, :] for i in range(16))
    rows = lax.fori_loop(0, 4, step, rows)
    return -jnp.concatenate(rows, 0)


def tree_kernel(
    right_h,
    guess_h,
    diag_h,
    lower_h,
    upper_h,
    inverse_h,
    basis_h,
    trans_h,
    mid_h,
    top_h,
    coup_h,
    base_o,
    left_o,
    out_o,
    cross_o,
    node_o,
    wide,
    pairs,
    right,
    guess,
    resid,
    sol,
    base,
    halo,
    halo2,
    basis,
    trans,
    expand,
    expand_halo,
    project,
    share,
    proj,
    proj_core,
    proj_z,
    chip,
    chip_in,
    pair_in,
    node_m,
    sx_in,
    sx_out,
    sz_in,
    group_m,
    q_out,
    xq_in,
    zq_out,
    zq_in,
    root_out,
    root_in,
    reduced,
    r1_in,
    v_out,
    r2_in,
    u_out,
    r3_in,
    gout,
    block_own,
    block_out,
    block_halo,
    load_sem,
    store_sem,
    send_sem,
    recv_sem,
):
    y = lax.axis_index("grp")
    l = lax.axis_index("leaf")
    core = l % 2
    j = l % 4
    z = (l // 2) % 4
    x = l // 8
    node = l // 4
    first = l - j
    index = y * 32 + l

    def at(place):
        place = place % 128
        return (place // 32, place % 32)

    nxt, prv = at(index + 1), at(index + 127)
    spots = [(j + d) % 4 for d in (1, 2, 3)]
    mates = [(y, first + spot) for spot in spots]
    twin = (y, l + 1 - 2 * core)
    mate_z = mates[1]
    x_spots = [(x + d) % 4 for d in (1, 2, 3)]
    cross = [(y, (l + 8 * d) % 32) for d in (1, 2, 3)]
    line = [(y, x * 8 + ((z + d) % 4) * 2 + core) for d in (1, 2, 3)]
    across_z = line[1]
    peers = [(y, (l + 4 * d) % 32) for d in range(1, 8)]
    peer_spots = [(node + d) % 8 for d in range(1, 8)]
    ring = [((y + d) % 4, l) for d in (1, 2, 3)]

    counter = [0]
    sent = []

    def remote(src, dst, device, start=True):
        k = counter[0]
        counter[0] += 1
        copy = pltpu.make_async_remote_copy(
            src_ref=src,
            dst_ref=dst,
            send_sem=send_sem.at[k],
            recv_sem=recv_sem.at[k],
            device_id=device,
            device_id_type=MESH,
        )
        if start:
            copy.start()
            sent.append(copy)
        return copy

    def arrived(*copies):
        for copy in copies:
            copy.wait_recv()

    local = []

    def load(src, dst):
        copy = pltpu.make_async_copy(src, dst, load_sem.at[len(local)])
        copy.start()
        local.append(copy)
        return copy

    load_share = [
        load(coup_h.at[0], share.at[0]),
        load(mid_h, share.at[1]),
        load(coup_h.at[pl.ds(1, 2)], share.at[pl.ds(2, 2)]),
        load(top_h, share.at[4]),
    ]
    load_inverse = load(inverse_h, wide.at[3])
    load_basis = load(basis_h, basis)
    load_trans = load(trans_h, trans)
    load_guess = load(guess_h, guess)
    load_diag = load(diag_h, wide.at[0])
    load_right = load(right_h, right)
    load_lower = load(lower_h, wide.at[1])
    load_upper = load(upper_h, wide.at[2])

    barrier = pltpu.get_barrier_semaphore()
    for device in [nxt, prv] + mates + peers + ring + line:
        pl.semaphore_signal(barrier, inc=1, device_id=device, device_id_type=MESH)

    @pl.when(j == 0)
    def _():
        for k in range(4):
            pl.semaphore_signal(
                barrier, inc=1, device_id=at(index + 124 + k), device_id_type=MESH
            )

    @pl.when(j == 3)
    def _():
        for k in range(4):
            pl.semaphore_signal(
                barrier, inc=1, device_id=at(index + 1 + k), device_id_type=MESH
            )

    pl.semaphore_wait(barrier, 20)

    def cols(c):
        return pl.ds(c * HALF, HALF)

    pieces = []

    def add_piece(src, dst, part):
        pieces.append(
            [
                remote(src.at[part], dst.at[(0,) + part], nxt, start=False),
                remote(src.at[part], dst.at[(1,) + part], prv, start=False),
            ]
        )
        return pieces[-1]

    def quarters(src, dst, c):
        return [add_piece(src, dst, (pl.ds(192 * q, 192), cols(c))) for q in range(4)]

    begun = [0]

    def pump(count):
        for _ in range(count):
            k = begun[0]
            if k >= 2:
                for copy in pieces[k - 2]:
                    copy.wait_send()
            for copy in pieces[k]:
                copy.start()
            begun[0] += 1

    halo_in = [quarters(guess_h, halo, c) for c in range(2)]
    expand_in = [
        add_piece(expand, expand_halo, (pl.ds(384 * q, 384), pl.ds(0, RANK))) for q in range(2)
    ]
    halo2_in = [quarters(sol, halo2, c) for c in range(2)]

    pump(2)

    for copy in load_share:
        copy.wait()
    half = pl.ds(pl.multiple_of(core * 64, 64), 64)
    other = pl.ds(pl.multiple_of(64 - core * 64, 64), 64)
    e1 = remote(share.at[:, other], chip_in, twin)

    def divide(m, scale=None):
        value = wide[m]
        if scale is not None:
            value = value * scale
        high, low = split(value)
        pairs[m, pl.ds(0, LEAF)] = high
        pairs[m, pl.ds(LEAF, LEAF)] = low

    load_inverse.wait()
    load_basis.wait()
    load_trans.wait()
    basis_t = basis[...].T
    trans_t = trans[...].T
    weighted = dot(wide[3], basis[...])
    proj[...] = dot(trans_t, dot(dot(basis_t, weighted), trans[...]))
    e_core = remote(proj, proj_core, twin)

    arrived(e1)
    chip[...] = share[:, half] + chip_in[...]
    e_pair = remote(chip.at[pl.ds(0, 2)], pair_in, mate_z)
    sx = [
        remote(chip.at[pl.ds(2, 3), pl.ds(x_spots[d] * 16, 16)], sx_in.at[d], cross[d])
        for d in range(3)
    ]
    arrived(e_core)
    proj_core[...] = proj[...] + proj_core[...]
    e_z = remote(proj_core, proj_z, mate_z)
    pump(2)

    expand[...] = dot(weighted, trans[...])
    high, low = split(dot(trans_t, basis_t))
    project[pl.ds(0, RANK)] = high
    project[pl.ds(RANK, RANK)] = low

    load_guess.wait()
    load_diag.wait()
    load_right.wait()
    divide(0)

    def own(c, carry):
        here = pl.ds(pl.multiple_of(c * HALF, HALF), HALF)
        resid[:, here] = right[:, here] - stacked(pairs.at[0], guess[:, here])
        return carry

    lax.fori_loop(0, 2, own, 0)

    arrived(e_pair)
    node_m[:, half] = chip[0:2] + pair_in[...]
    e_half = remote(node_m.at[:, half], node_m.at[:, half], twin)
    arrived(*sx)
    sx_own = pl.ds(pl.multiple_of(x * 16, 16), 16)
    sx_out[...] = chip[2:5, sx_own] + sx_in[0] + sx_in[1] + sx_in[2]
    sz = [remote(sx_out, sz_in.at[d], line[d]) for d in range(3)]
    arrived(e_z)
    arrived(e_half)
    p_proj, p_coup, p_mid = proj_core[...] + proj_z[...], node_m[0], node_m[1]
    pump(2)
    p_inv = spd_inverse(p_proj + p_coup)
    fm = dot(dot(p_inv, p_coup), p_mid)
    mf = fm.T
    q_out[...] = dot(mf, dot(p_proj, p_mid))
    xq = [remote(q_out.at[half], xq_in.at[d], cross[d]) for d in range(3)]

    arrived(*sz)
    group_rows = pl.ds(pl.multiple_of(core * 64 + x * 16, 16), 16)
    group_m[pl.ds(0, 3), group_rows] = sx_out[...] + sz_in[0] + sz_in[1] + sz_in[2]
    sx2 = [
        remote(group_m.at[pl.ds(0, 3), group_rows], group_m.at[pl.ds(0, 3), group_rows], cross[d])
        for d in range(3)
    ]
    pump(2)

    load_lower.wait()
    load_upper.wait()
    divide(1, jnp.where(index == 0, 0.0, 1.0))
    divide(2, jnp.where(index == 127, 0.0, 1.0))
    divide(3)

    def leaf_chunk(c):
        here = cols(c)
        for pair in halo_in[c]:
            arrived(*pair)

        def side(k, carry):
            resid[:, here] = resid[:, here] - stacked(pairs.at[k + 1], halo[k, :, here])
            return carry

        lax.fori_loop(0, 2, side, 0)
        sol[:, here] = stacked(pairs.at[3], resid[:, here])

    def reduce_chunk(c):
        here = cols(c)
        reduced[here, :] = stacked(project, sol[:, here]).T

    leaf_chunk(0)

    arrived(*xq)
    zq_out[...] = q_out[half] + xq_in[0] + xq_in[1] + xq_in[2]
    zq = remote(zq_out, zq_in, across_z)
    arrived(*sx2)
    s_half = remote(group_m.at[pl.ds(0, 3), half], group_m.at[pl.ds(0, 3), half], twin)
    pump(2)
    reduce_chunk(0)
    base[:, cols(0)] = guess[:, cols(0)] + sol[:, cols(0)]

    arrived(zq)
    group_m[3, half] = zq_out[...] + zq_in[...]
    g_half = remote(group_m.at[3, half], group_m.at[3, half], twin)

    leaf_chunk(1)
    reduce_chunk(1)
    r1 = [remote(reduced.at[pl.ds(spots[d] * 128, 128)], r1_in.at[d], mates[d]) for d in range(3)]
    pump(2)
    base[:, cols(1)] = guess[:, cols(1)] + sol[:, cols(1)]
    base_store = pltpu.make_async_copy(base, base_o, store_sem.at[0])
    base_store.start()

    arrived(s_half, g_half)
    g_coup, r_coup, g_top, g_proj = group_m[0], group_m[1], group_m[2], group_m[3]
    g_inv = spd_inverse(g_proj + g_coup)

    arrived(*r1)
    wide_rows = pl.ds(pl.multiple_of(j * 128, 128), 128)
    block_rhs = reduced[wide_rows] + r1_in[0] + r1_in[1] + r1_in[2]
    v_out[...] = dot(block_rhs, fm)
    r2 = [
        remote(v_out.at[pl.ds(peer_spots[d] * 16, 16)], r2_in.at[d], peers[d]) for d in range(7)
    ]
    ft = dot(dot(g_inv, g_coup), g_top)
    ft_t = ft.T
    root_out[...] = r_coup + dot(ft_t, dot(g_proj, g_top))
    to_root = [remote(root_out, root_in.at[d], ring[d]) for d in range(3)]
    pump(2)
    block_part = dot(block_rhs, p_inv)

    def again(c, carry):
        here = pl.ds(pl.multiple_of(c * HALF, HALF), HALF)
        resid[:, here] = resid[:, here] - stacked(pairs.at[0], sol[:, here])
        return carry

    lax.fori_loop(0, 2, again, 0)

    arrived(*r2)
    few_rows = pl.ds(pl.multiple_of(node * 16, 16), 16)
    group_rhs = v_out[few_rows]
    for d in range(7):
        group_rhs = group_rhs + r2_in[d]
    u_out[...] = dot(group_rhs, ft)
    r3 = [remote(u_out, r3_in.at[d], ring[d]) for d in range(3)]
    pump(2)
    group_part = dot(group_rhs, g_inv)

    arrived(*to_root)
    r_inv = spd_inverse(root_out[...] + root_in[0] + root_in[1] + root_in[2])
    down = dot(r_inv, ft_t)

    arrived(*r3)
    root_rhs = u_out[...] + r3_in[0] + r3_in[1] + r3_in[2]
    gout[few_rows] = group_part + dot(root_rhs, down)
    r4 = [remote(gout.at[few_rows], gout.at[few_rows], peers[d]) for d in range(7)]
    pump(2)

    def keep(ref, here, value):
        high, low = split(value)
        ref[0, :, here] = high
        ref[1, :, here] = low

    for pair in expand_in:
        arrived(*pair)
    every = pl.ds(0, RANK)
    keep(out_o, every, expand[...])
    keep(cross_o, every, stacked(pairs.at[0], expand[...]))
    for k in range(2):
        keep(cross_o, pl.ds((k + 1) * RANK, RANK), stacked(pairs.at[k + 1], expand_halo[k]))

    def sides(c):
        here = cols(c)
        for pair in halo2_in[c]:
            arrived(*pair)

        def side2(k, carry):
            resid[:, here] = resid[:, here] - stacked(pairs.at[k + 1], halo2[k, :, here])
            return carry

        lax.fori_loop(0, 2, side2, 0)

    sides(0)

    arrived(*r4)
    block_own[...] = block_part + dot(gout[...], mf)
    block_out[wide_rows] = block_own[...]
    r5 = [remote(block_own, block_out.at[wide_rows], mates[d]) for d in range(3)]
    k5 = counter[0]
    ahead = [at(index - j + 4), at(index - j + 127)]
    extra = [
        pltpu.make_async_remote_copy(
            src_ref=block_own,
            dst_ref=block_halo.at[wide_rows],
            send_sem=send_sem.at[k5 + way],
            recv_sem=recv_sem.at[k5 + 2 + j],
            device_id=ahead[way],
            device_id_type=MESH,
        )
        for way in range(2)
    ]
    for copy in extra:
        copy.start()

    sides(1)
    left_store = pltpu.make_async_copy(resid, left_o, store_sem.at[1])
    left_store.start()

    arrived(*r5)
    high, low = split(block_out[...].T)
    for k in range(3):
        node_o[0, pl.ds(k * RANK, RANK)] = high
        node_o[1, pl.ds(k * RANK, RANK)] = low

    def from_halo(k):
        for spot in range(4):
            pltpu.make_async_remote_copy(
                src_ref=block_own,
                dst_ref=block_halo.at[pl.ds(spot * 128, 128)],
                send_sem=send_sem.at[k5],
                recv_sem=recv_sem.at[k5 + 2 + spot],
                device_id=ahead[0],
                device_id_type=MESH,
            ).wait_recv()
        high, low = split(block_halo[...].T)
        node_o[0, pl.ds(k * RANK, RANK)] = high
        node_o[1, pl.ds(k * RANK, RANK)] = low

    @pl.when(j == 0)
    def _():
        from_halo(1)

    @pl.when(j == 3)
    def _():
        from_halo(2)

    for pair in pieces[-2:]:
        for copy in pair:
            copy.wait_send()
    for copy in sent + extra:
        copy.wait_send()
    base_store.wait()
    left_store.wait()


def last_kernel(base_ref, left_ref, out_ref, cross_ref, node_ref, guess_ref, resid_ref):
    def three(left, count):
        return (
            plain(left[0], node_ref[0, :count])
            + plain(left[1], node_ref[0, :count])
            + plain(left[0], node_ref[1, :count])
        )

    guess_ref[...] = base_ref[...] - three(out_ref, RANK)
    resid_ref[...] = left_ref[...] + three(cross_ref, 3 * RANK)


def tree(*args):
    any_spec = pl.BlockSpec(memory_space=pl.ANY)
    vmem = pl.BlockSpec(memory_space=pltpu.VMEM)

    def buf(*shape, dtype=F32):
        return pltpu.VMEM(shape, dtype)

    scratch = [
        buf(4, LEAF, LEAF),
        buf(4, 2 * LEAF, LEAF, dtype=BF16),
        buf(LEAF, RHS),
        buf(LEAF, RHS),
        buf(LEAF, RHS),
        buf(LEAF, RHS),
        buf(LEAF, RHS),
        buf(2, LEAF, RHS),
        buf(2, LEAF, RHS),
        buf(LEAF, RANK),
        buf(RANK, RANK),
        buf(LEAF, RANK),
        buf(2, LEAF, RANK),
        buf(2 * RANK, LEAF, dtype=BF16),
        buf(5, RANK, RANK),
        buf(RANK, RANK),
        buf(RANK, RANK),
        buf(RANK, RANK),
        buf(5, 64, RANK),
        buf(5, 64, RANK),
        buf(2, 64, RANK),
        buf(2, RANK, RANK),
        buf(3, 3, 16, RANK),
        buf(3, 16, RANK),
        buf(3, 3, 16, RANK),
        buf(4, RANK, RANK),
        buf(RANK, RANK),
        buf(3, 64, RANK),
        buf(64, RANK),
        buf(64, RANK),
        buf(RANK, RANK),
        buf(3, RANK, RANK),
        buf(RHS, RANK),
        buf(3, RANK, RANK),
        buf(RANK, RANK),
        buf(7, 16, RANK),
        buf(16, RANK),
        buf(3, 16, RANK),
        buf(RANK, RANK),
        buf(RANK, RANK),
        buf(RHS, RANK),
        buf(RHS, RANK),
        pltpu.SemaphoreType.DMA((12,)),
        pltpu.SemaphoreType.DMA((2,)),
        pltpu.SemaphoreType.DMA((96,)),
        pltpu.SemaphoreType.DMA((96,)),
    ]
    base, left, out, cross, node = pl.pallas_call(
        tree_kernel,
        out_shape=[
            jax.ShapeDtypeStruct((LEAF, RHS), F32),
            jax.ShapeDtypeStruct((LEAF, RHS), F32),
            jax.ShapeDtypeStruct((2, LEAF, RANK), BF16),
            jax.ShapeDtypeStruct((2, LEAF, 3 * RANK), BF16),
            jax.ShapeDtypeStruct((2, 3 * RANK, RHS), BF16),
        ],
        in_specs=[any_spec] * 11,
        out_specs=[any_spec, any_spec, vmem, vmem, vmem],
        scratch_shapes=scratch,
        compiler_params=pltpu.CompilerParams(
            collective_id=0, has_side_effects=True, vmem_limit_bytes=56 * 2**20
        ),
    )(*args)
    block = 128
    return pl.pallas_call(
        last_kernel,
        grid=(LEAF // block,),
        in_specs=[
            pl.BlockSpec((block, RHS), lambda i: (i, 0)),
            pl.BlockSpec((block, RHS), lambda i: (i, 0)),
            pl.BlockSpec((2, block, RANK), lambda i: (0, i, 0)),
            pl.BlockSpec((2, block, 3 * RANK), lambda i: (0, i, 0)),
            pl.BlockSpec((2, 3 * RANK, RHS), lambda i: (0, 0, 0)),
        ],
        out_specs=[
            pl.BlockSpec((block, RHS), lambda i: (i, 0)),
            pl.BlockSpec((block, RHS), lambda i: (i, 0)),
        ],
        out_shape=[jax.ShapeDtypeStruct((LEAF, RHS), F32)] * 2,
    )(base, left, out, cross, node)


def body(
    right_side,
    guess,
    near_diag,
    near_lower,
    near_upper,
    leaf_inverse,
    leaf_basis,
    leaf_transfer,
    mid_share,
    top_share,
    coupling_share,
):
    new_guess, new_residual = tree(
        right_side,
        guess,
        near_diag[0],
        near_lower[0],
        near_upper[0],
        leaf_inverse[0],
        leaf_basis[0],
        leaf_transfer[0],
        mid_share[0],
        top_share[0],
        coupling_share[0],
    )
    return (new_guess, new_residual)


def solution(mesh):
    field = P(("grp", "leaf"), None)
    block = P(("grp", "leaf"), None, None)
    shares = P(("grp", "leaf"), None, None, None)
    in_specs = (field, field) + (block,) * 8 + (shares,)
    return jax.shard_map(
        body, mesh=mesh, in_specs=in_specs, out_specs=(field, field), check_vma=False
    )
```

time: 113 us -> 86.8 us (0.77)
  Pallas kernels: 111 us -> 86 us
    pallas_call x1, Pallas kernels: 105 us -> 79.3 us  [tree(): pl.pallas_call(tree_kernel, out_shape=[jax.ShapeDtypeStruct((LEAF, RHS),...]
where the time goes in v2:
time: 86.8 us; the launch traced here: 86.6 us
  Pallas kernels  86 us (99%)
    pallas_call x1, Pallas kernels, tree(): pl.pallas_call(tree_kernel, out_shape=[jax.ShapeDtypeStruct((LEAF, RHS),...  79.3 us
    pallas_call x1, Pallas kernels, tree(): pl.pallas_call(last_kernel, grid=(LEAF // block,), in_specs=[pl.BlockSpec...  6.66 us

profile of v2, /device:TPU:33, one launch (start us, length us, event | category | flops | bytes accessed | tf_op | source)
XLA Modules:
  0.0 86.6 jit_solution(9025548315111122953)
XLA Ops:
  0.6 79.3 %shard_map.122 = (f32[768,512]{1,0:T(8,128)}, f32[768,512]{1,0:T(8,128)}, bf16[2,768,128]{2,1,0:T(8,128)(2,1)}, bf16[2,768,384]{2,1,0:T(8,128)(2,1)}, bf16[2,384,512]{2,1,0:T(8,128)(2,1)}) custom-call(f32[768,512]{1,0:T(8,128)} %right_h.1, f32[768,512]{1,0:T(8,128)} %guess_h.1, f32[768,768]{1,0:T(8,128)} %bitcast.9, f32[768,768]{1,0:T(8,128)} %bitcast.10, ...), custom_call_target="tpu_custom_call" | custom-call | tf_op jit(solution)/shard_map/pallas_call | solution.py:627
  80.0 6.7 %shard_map.123 = (f32[768,512]{1,0:T(8,128)}, f32[768,512]{1,0:T(8,128)}) custom-call(f32[768,512]{1,0:T(8,128)} %get-tuple-element.7.base_ref, f32[768,512]{1,0:T(8,128)} %get-tuple-element.8.left_ref, bf16[2,768,128]{2,1,0:T(8,128)(2,1)} %get-tuple-element.9.out_ref, bf16[2,768,384]{2,1,0:T(8,128)(2,1)} %get-tuple-element.10.cross_ref, ...), custom_call_target="tpu_custom_call" | custom-call | tf_op jit(solution)/shard_map/pallas_call | solution.py:644

commit v3 on v2

--- a/solution.py
+++ b/solution.py
@@ -141,7 +141,7 @@
     project,
     share,
     proj,
-    proj_core,
+    proj_in,
     proj_z,
     chip,
     chip_in,
@@ -158,11 +158,15 @@
     root_out,
     root_in,
     reduced,
+    reduced_in,
     r1_in,
+    kept,
+    block_rhs,
     v_out,
     r2_in,
     u_out,
     r3_in,
+    part,
     gout,
     block_own,
     block_out,
@@ -177,6 +181,7 @@
     core = l % 2
     j = l % 4
     z = (l // 2) % 4
+    zp = z % 2
     x = l // 8
     node = l // 4
     first = l - j
@@ -186,23 +191,28 @@
         place = place % 128
         return (place // 32, place % 32)
 
-    nxt, prv = at(index + 1), at(index + 127)
-    spots = [(j + d) % 4 for d in (1, 2, 3)]
-    mates = [(y, first + spot) for spot in spots]
+    def on(which):
+        return pl.when(core == which)
+
     twin = (y, l + 1 - 2 * core)
-    mate_z = mates[1]
+    up = at(index + 1)
+    down_chip = at(index + 126)
+    up_chip = at(index + 2)
+    before = at(index + 127)
+    mate_z = (y, first + core + 2 - 2 * zp)
+    mate_z1 = (y, first + 3 - 2 * zp)
     x_spots = [(x + d) % 4 for d in (1, 2, 3)]
     cross = [(y, (l + 8 * d) % 32) for d in (1, 2, 3)]
     line = [(y, x * 8 + ((z + d) % 4) * 2 + core) for d in (1, 2, 3)]
-    across_z = line[1]
     peers = [(y, (l + 4 * d) % 32) for d in range(1, 8)]
     peer_spots = [(node + d) % 8 for d in range(1, 8)]
     ring = [((y + d) % 4, l) for d in (1, 2, 3)]
+    ahead = [at(index - j + 4), at(index - j + 127)]
 
     counter = [0]
-    sent = []
-
-    def remote(src, dst, device, start=True):
+    sent = {0: [], 1: []}
+
+    def message(src, dst, device, which):
         k = counter[0]
         counter[0] += 1
         copy = pltpu.make_async_remote_copy(
@@ -213,10 +223,12 @@
             device_id=device,
             device_id_type=MESH,
         )
-        if start:
+        sent[which].append(copy)
+        return copy
+
+    def begin(*copies):
+        for copy in copies:
             copy.start()
-            sent.append(copy)
-        return copy
 
     def arrived(*copies):
         for copy in copies:
@@ -230,15 +242,15 @@
         local.append(copy)
         return copy
 
+    load_inverse = load(inverse_h, wide.at[3])
+    load_basis = load(basis_h, basis)
+    load_trans = load(trans_h, trans)
     load_share = [
         load(coup_h.at[0], share.at[0]),
         load(mid_h, share.at[1]),
         load(coup_h.at[pl.ds(1, 2)], share.at[pl.ds(2, 2)]),
         load(top_h, share.at[4]),
     ]
-    load_inverse = load(inverse_h, wide.at[3])
-    load_basis = load(basis_h, basis)
-    load_trans = load(trans_h, trans)
     load_guess = load(guess_h, guess)
     load_diag = load(diag_h, wide.at[0])
     load_right = load(right_h, right)
@@ -246,67 +258,136 @@
     load_upper = load(upper_h, wide.at[2])
 
     barrier = pltpu.get_barrier_semaphore()
-    for device in [nxt, prv] + mates + peers + ring + line:
+
+    def hello(device):
         pl.semaphore_signal(barrier, inc=1, device_id=device, device_id_type=MESH)
 
+    @on(1)
+    def _():
+        for device in (twin, up_chip, (y, first + 2 - 2 * zp)):
+            hello(device)
+
+    @on(0)
+    def _():
+        for device in [twin, before] + line + cross + peers + ring:
+            hello(device)
+
     @pl.when(j == 0)
     def _():
-        for k in range(4):
-            pl.semaphore_signal(
-                barrier, inc=1, device_id=at(index + 124 + k), device_id_type=MESH
-            )
+        hello(at(index + 124))
+        hello(at(index + 126))
 
     @pl.when(j == 3)
     def _():
-        for k in range(4):
-            pl.semaphore_signal(
-                barrier, inc=1, device_id=at(index + 1 + k), device_id_type=MESH
-            )
-
-    pl.semaphore_wait(barrier, 20)
+        hello(at(index + 1))
+        hello(at(index + 3))
+
+    @on(1)
+    def _():
+        pl.semaphore_wait(barrier, 3)
+
+    @on(0)
+    def _():
+        pl.semaphore_wait(barrier, 20)
 
     def cols(c):
         return pl.ds(c * HALF, HALF)
 
-    pieces = []
-
-    def add_piece(src, dst, part):
-        pieces.append(
-            [
-                remote(src.at[part], dst.at[(0,) + part], nxt, start=False),
-                remote(src.at[part], dst.at[(1,) + part], prv, start=False),
-            ]
+    class Part:
+        def __init__(self, src, dst, place):
+            low, high = dst.at[(0,) + place], dst.at[(1,) + place]
+            self.low = message(src.at[place], low, twin, 0)
+            k = counter[0]
+            counter[0] += 3
+
+            def one(src, dst, device, send, recv):
+                copy = pltpu.make_async_remote_copy(
+                    src_ref=src,
+                    dst_ref=dst,
+                    send_sem=send_sem.at[send],
+                    recv_sem=recv_sem.at[recv],
+                    device_id=device,
+                    device_id_type=MESH,
+                )
+                sent[1].append(copy)
+                return copy
+
+            self.high = one(src.at[place], high, twin, k, k)
+            self.up = one(src.at[place], low, up, k + 1, k - 1)
+            self.down = one(low, high, down_chip, k + 2, k)
+
+    def quarters(src, dst, c):
+        return [Part(src, dst, (pl.ds(192 * q, 192), cols(c))) for q in range(4)]
+
+    halo_in = quarters(guess_h, halo, 0) + quarters(guess_h, halo, 1)
+    whole = pl.ds(0, LEAF)
+    expand_in = Part(expand, expand_halo, (whole, pl.ds(0, RANK)))
+    halo2_in = [Part(sol, halo2, (whole, cols(c))) for c in range(2)]
+
+    e1 = message(share, chip_in, twin, 1)
+    e_core = message(proj, proj_in, twin, 1)
+
+    @on(1)
+    def _():
+        begin(halo_in[0].up, halo_in[0].high)
+        for copy in load_share:
+            copy.wait()
+        begin(e1, halo_in[1].up, halo_in[1].high)
+        for k in range(2):
+            arrived(halo_in[k].low)
+            begin(halo_in[k].down)
+
+    @on(0)
+    def _():
+        for piece in halo_in:
+            begin(piece.low)
+
+    load_inverse.wait()
+    load_basis.wait()
+    load_trans.wait()
+    basis_t = basis[...].T
+    trans_t = trans[...].T
+    weighted = dot(wide[3], basis[...])
+    proj[...] = dot(trans_t, dot(dot(basis_t, weighted), trans[...]))
+
+    @on(1)
+    def _():
+        begin(e_core)
+        for piece in halo_in[2:]:
+            begin(piece.up, piece.high)
+            arrived(piece.low)
+            begin(piece.down)
+
+    x_rows = pl.ds(pl.multiple_of(x * 32, 32), 32)
+    e_pair = message(chip.at[pl.ds(0, 2)], pair_in, mate_z, 0)
+    sx = [
+        message(chip.at[pl.ds(2, 3), pl.ds(x_spots[d] * 32, 32)], sx_in.at[d], cross[d], 0)
+        for d in range(3)
+    ]
+    sz = [message(sx_out, sz_in.at[d], line[d], 0) for d in range(3)]
+    sx2 = [
+        message(
+            group_m.at[pl.ds(0, 3), x_rows], group_m.at[pl.ds(0, 3), x_rows], cross[d], 0
         )
-        return pieces[-1]
-
-    def quarters(src, dst, c):
-        return [add_piece(src, dst, (pl.ds(192 * q, 192), cols(c))) for q in range(4)]
-
-    begun = [0]
-
-    def pump(count):
-        for _ in range(count):
-            k = begun[0]
-            if k >= 2:
-                for copy in pieces[k - 2]:
-                    copy.wait_send()
-            for copy in pieces[k]:
-                copy.start()
-            begun[0] += 1
-
-    halo_in = [quarters(guess_h, halo, c) for c in range(2)]
-    expand_in = [
-        add_piece(expand, expand_halo, (pl.ds(384 * q, 384), pl.ds(0, RANK))) for q in range(2)
+        for d in range(3)
     ]
-    halo2_in = [quarters(sol, halo2, c) for c in range(2)]
-
-    pump(2)
-
-    for copy in load_share:
-        copy.wait()
-    half = pl.ds(pl.multiple_of(core * 64, 64), 64)
-    other = pl.ds(pl.multiple_of(64 - core * 64, 64), 64)
-    e1 = remote(share.at[:, other], chip_in, twin)
+    e_z = message(proj, proj_z, mate_z, 0)
+
+    @on(0)
+    def _():
+        for copy in load_share:
+            copy.wait()
+        arrived(e1)
+        chip[...] = share[...] + chip_in[...]
+        begin(e_pair, *sx)
+        arrived(e_core)
+        proj[...] = proj[...] + proj_in[...]
+        begin(e_z)
+
+    expand[...] = dot(weighted, trans[...])
+    high, low = split(dot(trans_t, basis_t))
+    project[pl.ds(0, RANK)] = high
+    project[pl.ds(RANK, RANK)] = low
 
     def divide(m, scale=None):
         value = wide[m]
@@ -316,32 +397,6 @@
         pairs[m, pl.ds(0, LEAF)] = high
         pairs[m, pl.ds(LEAF, LEAF)] = low
 
-    load_inverse.wait()
-    load_basis.wait()
-    load_trans.wait()
-    basis_t = basis[...].T
-    trans_t = trans[...].T
-    weighted = dot(wide[3], basis[...])
-    proj[...] = dot(trans_t, dot(dot(basis_t, weighted), trans[...]))
-    e_core = remote(proj, proj_core, twin)
-
-    arrived(e1)
-    chip[...] = share[:, half] + chip_in[...]
-    e_pair = remote(chip.at[pl.ds(0, 2)], pair_in, mate_z)
-    sx = [
-        remote(chip.at[pl.ds(2, 3), pl.ds(x_spots[d] * 16, 16)], sx_in.at[d], cross[d])
-        for d in range(3)
-    ]
-    arrived(e_core)
-    proj_core[...] = proj[...] + proj_core[...]
-    e_z = remote(proj_core, proj_z, mate_z)
-    pump(2)
-
-    expand[...] = dot(weighted, trans[...])
-    high, low = split(dot(trans_t, basis_t))
-    project[pl.ds(0, RANK)] = high
-    project[pl.ds(RANK, RANK)] = low
-
     load_guess.wait()
     load_diag.wait()
     load_right.wait()
@@ -354,31 +409,29 @@
 
     lax.fori_loop(0, 2, own, 0)
 
-    arrived(e_pair)
-    node_m[:, half] = chip[0:2] + pair_in[...]
-    e_half = remote(node_m.at[:, half], node_m.at[:, half], twin)
-    arrived(*sx)
-    sx_own = pl.ds(pl.multiple_of(x * 16, 16), 16)
-    sx_out[...] = chip[2:5, sx_own] + sx_in[0] + sx_in[1] + sx_in[2]
-    sz = [remote(sx_out, sz_in.at[d], line[d]) for d in range(3)]
-    arrived(e_z)
-    arrived(e_half)
-    p_proj, p_coup, p_mid = proj_core[...] + proj_z[...], node_m[0], node_m[1]
-    pump(2)
-    p_inv = spd_inverse(p_proj + p_coup)
-    fm = dot(dot(p_inv, p_coup), p_mid)
-    mf = fm.T
-    q_out[...] = dot(mf, dot(p_proj, p_mid))
-    xq = [remote(q_out.at[half], xq_in.at[d], cross[d]) for d in range(3)]
-
-    arrived(*sz)
-    group_rows = pl.ds(pl.multiple_of(core * 64 + x * 16, 16), 16)
-    group_m[pl.ds(0, 3), group_rows] = sx_out[...] + sz_in[0] + sz_in[1] + sz_in[2]
-    sx2 = [
-        remote(group_m.at[pl.ds(0, 3), group_rows], group_m.at[pl.ds(0, 3), group_rows], cross[d])
-        for d in range(3)
-    ]
-    pump(2)
+    xq = [message(q_out, xq_in.at[d], cross[d], 0) for d in range(3)]
+
+    @on(0)
+    def _():
+        begin(expand_in.low)
+        arrived(*sx)
+        sx_out[...] = chip[2:5, x_rows] + sx_in[0] + sx_in[1] + sx_in[2]
+        begin(*sz)
+        arrived(e_pair)
+        node_m[...] = chip[0:2] + pair_in[...]
+        arrived(e_z)
+        p_proj, p_coup, p_mid = proj[...] + proj_z[...], node_m[0], node_m[1]
+        p_inv = spd_inverse(p_proj + p_coup)
+        fm = dot(dot(p_inv, p_coup), p_mid)
+        mf = fm.T
+        q_out[...] = dot(mf, dot(p_proj, p_mid))
+        begin(*xq)
+        kept[0] = p_inv
+        kept[1] = fm
+        kept[2] = mf
+        arrived(*sz)
+        group_m[pl.ds(0, 3), x_rows] = sx_out[...] + sz_in[0] + sz_in[1] + sz_in[2]
+        begin(*sx2)
 
     load_lower.wait()
     load_upper.wait()
@@ -388,8 +441,13 @@
 
     def leaf_chunk(c):
         here = cols(c)
-        for pair in halo_in[c]:
-            arrived(*pair)
+        for piece in halo_in[4 * c : 4 * c + 4]:
+            arrived(piece.high)
+
+        @on(0)
+        def _():
+            for piece in halo_in[4 * c : 4 * c + 4]:
+                arrived(piece.low)
 
         def side(k, carry):
             resid[:, here] = resid[:, here] - stacked(pairs.at[k + 1], halo[k, :, here])
@@ -402,46 +460,76 @@
         here = cols(c)
         reduced[here, :] = stacked(project, sol[:, here]).T
 
+    to_core = [message(reduced.at[cols(c)], reduced_in.at[cols(c)], twin, 1) for c in range(2)]
+
     leaf_chunk(0)
-
-    arrived(*xq)
-    zq_out[...] = q_out[half] + xq_in[0] + xq_in[1] + xq_in[2]
-    zq = remote(zq_out, zq_in, across_z)
-    arrived(*sx2)
-    s_half = remote(group_m.at[pl.ds(0, 3), half], group_m.at[pl.ds(0, 3), half], twin)
-    pump(2)
     reduce_chunk(0)
+
+    @on(1)
+    def _():
+        begin(to_core[0], expand_in.up, expand_in.high)
+        arrived(expand_in.low)
+        begin(expand_in.down, halo2_in[0].high)
+
+    zq = message(zq_out, zq_in, line[1], 0)
+
+    @on(0)
+    def _():
+        begin(halo2_in[0].low)
+        arrived(*xq)
+        zq_out[...] = q_out[...] + xq_in[0] + xq_in[1] + xq_in[2]
+        begin(zq)
+
     base[:, cols(0)] = guess[:, cols(0)] + sol[:, cols(0)]
-
-    arrived(zq)
-    group_m[3, half] = zq_out[...] + zq_in[...]
-    g_half = remote(group_m.at[3, half], group_m.at[3, half], twin)
-
     leaf_chunk(1)
     reduce_chunk(1)
-    r1 = [remote(reduced.at[pl.ds(spots[d] * 128, 128)], r1_in.at[d], mates[d]) for d in range(3)]
-    pump(2)
+
+    @on(1)
+    def _():
+        begin(to_core[1], halo2_in[0].up)
+        arrived(halo2_in[0].low)
+        begin(halo2_in[0].down, halo2_in[1].high, halo2_in[1].up)
+        arrived(halo2_in[1].low)
+        begin(halo2_in[1].down)
+
+    half = pl.ds(pl.multiple_of(zp * 256, 256), 256)
+    other = pl.ds(pl.multiple_of(256 - zp * 256, 256), 256)
+    r1 = message(reduced.at[other], r1_in, mate_z, 0)
+    to_root = [message(root_out, root_in.at[d], ring[d], 0) for d in range(3)]
+    r2 = [
+        message(v_out.at[pl.ds(peer_spots[d] * 32, 32)], r2_in.at[d], peers[d], 0)
+        for d in range(7)
+    ]
+
+    @on(0)
+    def _():
+        begin(halo2_in[1].low)
+        arrived(*to_core)
+        reduced[...] = reduced[...] + reduced_in[...]
+        begin(r1)
+
     base[:, cols(1)] = guess[:, cols(1)] + sol[:, cols(1)]
     base_store = pltpu.make_async_copy(base, base_o, store_sem.at[0])
     base_store.start()
 
-    arrived(s_half, g_half)
-    g_coup, r_coup, g_top, g_proj = group_m[0], group_m[1], group_m[2], group_m[3]
-    g_inv = spd_inverse(g_proj + g_coup)
-
-    arrived(*r1)
-    wide_rows = pl.ds(pl.multiple_of(j * 128, 128), 128)
-    block_rhs = reduced[wide_rows] + r1_in[0] + r1_in[1] + r1_in[2]
-    v_out[...] = dot(block_rhs, fm)
-    r2 = [
-        remote(v_out.at[pl.ds(peer_spots[d] * 16, 16)], r2_in.at[d], peers[d]) for d in range(7)
-    ]
-    ft = dot(dot(g_inv, g_coup), g_top)
-    ft_t = ft.T
-    root_out[...] = r_coup + dot(ft_t, dot(g_proj, g_top))
-    to_root = [remote(root_out, root_in.at[d], ring[d]) for d in range(3)]
-    pump(2)
-    block_part = dot(block_rhs, p_inv)
+    @on(0)
+    def _():
+        arrived(*sx2)
+        arrived(zq)
+        g_coup, r_coup, g_top = group_m[0], group_m[1], group_m[2]
+        g_proj = zq_out[...] + zq_in[...]
+        g_inv = spd_inverse(g_proj + g_coup)
+        arrived(r1)
+        block_rhs[...] = reduced[half] + r1_in[...]
+        v_out[...] = dot(block_rhs[...], kept[1])
+        begin(*r2)
+        ft = dot(dot(g_inv, g_coup), g_top)
+        ft_t = ft.T
+        root_out[...] = r_coup + dot(ft_t, dot(g_proj, g_top))
+        begin(*to_root)
+        kept[3] = g_inv
+        kept[4] = ft
+        kept[5] = ft_t
 
     def again(c, carry):
         here = pl.ds(pl.multiple_of(c * HALF, HALF), HALF)
@@ -450,43 +538,50 @@
 
     lax.fori_loop(0, 2, again, 0)
 
-    arrived(*r2)
-    few_rows = pl.ds(pl.multiple_of(node * 16, 16), 16)
-    group_rhs = v_out[few_rows]
-    for d in range(7):
-        group_rhs = group_rhs + r2_in[d]
-    u_out[...] = dot(group_rhs, ft)
-    r3 = [remote(u_out, r3_in.at[d], ring[d]) for d in range(3)]
-    pump(2)
-    group_part = dot(group_rhs, g_inv)
-
-    arrived(*to_root)
-    r_inv = spd_inverse(root_out[...] + root_in[0] + root_in[1] + root_in[2])
-    down = dot(r_inv, ft_t)
-
-    arrived(*r3)
-    root_rhs = u_out[...] + r3_in[0] + r3_in[1] + r3_in[2]
-    gout[few_rows] = group_part + dot(root_rhs, down)
-    r4 = [remote(gout.at[few_rows], gout.at[few_rows], peers[d]) for d in range(7)]
-    pump(2)
+    few_rows = pl.ds(pl.multiple_of(node * 32, 32), 32)
+    r3 = [message(u_out, r3_in.at[d], ring[d], 0) for d in range(3)]
+    r4 = [message(gout.at[few_rows], gout.at[few_rows], peers[d], 0) for d in range(7)]
+
+    @on(0)
+    def _():
+        arrived(*r2)
+        group_rhs = v_out[few_rows]
+        for d in range(7):
+            group_rhs = group_rhs + r2_in[d]
+        u_out[...] = dot(group_rhs, kept[4])
+        begin(*r3)
+        part[...] = dot(group_rhs, kept[3])
+        arrived(*to_root)
+        r_inv = spd_inverse(root_out[...] + root_in[0] + root_in[1] + root_in[2])
+        down = dot(r_inv, kept[5])
+        arrived(*r3)
+        root_rhs = u_out[...] + r3_in[0] + r3_in[1] + r3_in[2]
+        gout[few_rows] = part[...] + dot(root_rhs, down)
+        begin(*r4)
 
     def keep(ref, here, value):
         high, low = split(value)
         ref[0, :, here] = high
         ref[1, :, here] = low
 
-    for pair in expand_in:
-        arrived(*pair)
-    every = pl.ds(0, RANK)
-    keep(out_o, every, expand[...])
-    keep(cross_o, every, stacked(pairs.at[0], expand[...]))
+    arrived(expand_in.high)
+
+    @on(0)
+    def _():
+        arrived(expand_in.low)
+
+    keep(out_o, pl.ds(0, RANK), expand[...])
+    keep(cross_o, pl.ds(0, RANK), stacked(pairs.at[0], expand[...]))
     for k in range(2):
         keep(cross_o, pl.ds((k + 1) * RANK, RANK), stacked(pairs.at[k + 1], expand_halo[k]))
 
     def sides(c):
         here = cols(c)
-        for pair in halo2_in[c]:
-            arrived(*pair)
+        arrived(halo2_in[c].high)
+
+        @on(0)
+        def _():
+            arrived(halo2_in[c].low)
 
         def side2(k, carry):
             resid[:, here] = resid[:, here] - stacked(pairs.at[k + 1], halo2[k, :, here])
@@ -496,43 +591,53 @@
 
     sides(0)
 
-    arrived(*r4)
-    block_own[...] = block_part + dot(gout[...], mf)
-    block_out[wide_rows] = block_own[...]
-    r5 = [remote(block_own, block_out.at[wide_rows], mates[d]) for d in range(3)]
+    r5 = message(block_own, block_out.at[half], mate_z, 0)
+    r5_twin = message(block_own, block_out.at[half], twin, 0)
+    r5_far = message(block_own, block_out.at[half], mate_z1, 0)
     k5 = counter[0]
-    ahead = [at(index - j + 4), at(index - j + 127)]
     extra = [
         pltpu.make_async_remote_copy(
             src_ref=block_own,
-            dst_ref=block_halo.at[wide_rows],
+            dst_ref=block_halo.at[half],
             send_sem=send_sem.at[k5 + way],
-            recv_sem=recv_sem.at[k5 + 2 + j],
+            recv_sem=recv_sem.at[k5 + zp],
             device_id=ahead[way],
             device_id_type=MESH,
         )
         for way in range(2)
     ]
-    for copy in extra:
-        copy.start()
+
+    @on(0)
+    def _():
+        arrived(*r4)
+        block_own[...] = dot(block_rhs[...], kept[0]) + dot(gout[...], kept[2])
+        begin(r5, r5_far, r5_twin, *extra)
+        block_out[half] = block_own[...]
 
     sides(1)
     left_store = pltpu.make_async_copy(resid, left_o, store_sem.at[1])
     left_store.start()
 
-    arrived(*r5)
+    @on(0)
+    def _():
+        arrived(r5)
+
+    @on(1)
+    def _():
+        arrived(r5_twin, r5_far)
+
     high, low = split(block_out[...].T)
     for k in range(3):
         node_o[0, pl.ds(k * RANK, RANK)] = high
         node_o[1, pl.ds(k * RANK, RANK)] = low
 
     def from_halo(k):
-        for spot in range(4):
+        for spot in range(2):
             pltpu.make_async_remote_copy(
                 src_ref=block_own,
-                dst_ref=block_halo.at[pl.ds(spot * 128, 128)],
+                dst_ref=block_halo.at[pl.ds(spot * 256, 256)],
                 send_sem=send_sem.at[k5],
-                recv_sem=recv_sem.at[k5 + 2 + spot],
+                recv_sem=recv_sem.at[k5 + spot],
                 device_id=ahead[0],
                 device_id_type=MESH,
             ).wait_recv()
@@ -548,11 +653,16 @@
     def _():
         from_halo(2)
 
-    for pair in pieces[-2:]:
-        for copy in pair:
-            copy.wait_send()
-    for copy in sent + extra:
-        copy.wait_send()
+    for which in range(2):
+
+        @on(which)
+        def _():
+            for copy in sent[which]:
+                copy.wait_send()
+            if which == 0:
+                for copy in extra:
+                    copy.wait_send()
+
     base_store.wait()
     left_store.wait()
 
@@ -595,34 +705,38 @@
         buf(RANK, RANK),
         buf(RANK, RANK),
         buf(RANK, RANK),
-        buf(5, 64, RANK),
-        buf(5, 64, RANK),
-        buf(2, 64, RANK),
+        buf(5, RANK, RANK),
+        buf(5, RANK, RANK),
         buf(2, RANK, RANK),
-        buf(3, 3, 16, RANK),
-        buf(3, 16, RANK),
-        buf(3, 3, 16, RANK),
-        buf(4, RANK, RANK),
+        buf(2, RANK, RANK),
+        buf(3, 3, 32, RANK),
+        buf(3, 32, RANK),
+        buf(3, 3, 32, RANK),
+        buf(3, RANK, RANK),
         buf(RANK, RANK),
-        buf(3, 64, RANK),
-        buf(64, RANK),
-        buf(64, RANK),
+        buf(3, RANK, RANK),
+        buf(RANK, RANK),
+        buf(RANK, RANK),
         buf(RANK, RANK),
         buf(3, RANK, RANK),
         buf(RHS, RANK),
-        buf(3, RANK, RANK),
-        buf(RANK, RANK),
-        buf(7, 16, RANK),
-        buf(16, RANK),
-        buf(3, 16, RANK),
-        buf(RANK, RANK),
-        buf(RANK, RANK),
+        buf(RHS, RANK),
+        buf(HALF, RANK),
+        buf(6, RANK, RANK),
+        buf(HALF, RANK),
+        buf(HALF, RANK),
+        buf(7, 32, RANK),
+        buf(32, RANK),
+        buf(3, 32, RANK),
+        buf(32, RANK),
+        buf(HALF, RANK),
+        buf(HALF, RANK),
         buf(RHS, RANK),
         buf(RHS, RANK),
         pltpu.SemaphoreType.DMA((12,)),
         pltpu.SemaphoreType.DMA((2,)),
-        pltpu.SemaphoreType.DMA((96,)),
-        pltpu.SemaphoreType.DMA((96,)),
+        pltpu.SemaphoreType.DMA((112,)),
+        pltpu.SemaphoreType.DMA((112,)),
     ]
     base, left, out, cross, node = pl.pallas_call(
         tree_kernel,

time: 86.8 us -> 89 us (1.025)
  Pallas kernels: 86 us -> 88.1 us
    pallas_call x1, Pallas kernels: 79.3 us -> 81.5 us  [tree(): pl.pallas_call(tree_kernel, out_shape=[jax.ShapeDtypeStruct((LEAF, RHS),...]
where the time goes in v3:
time: 89 us; the launch traced here: 88.8 us
  Pallas kernels  88.1 us (99%)
    pallas_call x1, Pallas kernels, tree(): pl.pallas_call(tree_kernel, out_shape=[jax.ShapeDtypeStruct((LEAF, RHS),...  81.5 us
    pallas_call x1, Pallas kernels, tree(): pl.pallas_call(last_kernel, grid=(LEAF // block,), in_specs=[pl.BlockSpec...  6.65 us

profile of v3, /device:TPU:33, one launch (start us, length us, event | category | flops | bytes accessed | tf_op | source)
XLA Modules:
  0.0 88.8 jit_solution(17587444078621247635)
XLA Ops:
  0.6 81.5 %shard_map.122 = (f32[768,512]{1,0:T(8,128)}, f32[768,512]{1,0:T(8,128)}, bf16[2,768,128]{2,1,0:T(8,128)(2,1)}, bf16[2,768,384]{2,1,0:T(8,128)(2,1)}, bf16[2,384,512]{2,1,0:T(8,128)(2,1)}) custom-call(f32[768,512]{1,0:T(8,128)} %right_h.1, f32[768,512]{1,0:T(8,128)} %guess_h.1, f32[768,768]{1,0:T(8,128)} %bitcast.9, f32[768,768]{1,0:T(8,128)} %bitcast.10, ...), custom_call_target="tpu_custom_call" | custom-call | tf_op jit(solution)/shard_map/pallas_call | solution.py:741
  82.1 6.7 %shard_map.123 = (f32[768,512]{1,0:T(8,128)}, f32[768,512]{1,0:T(8,128)}) custom-call(f32[768,512]{1,0:T(8,128)} %get-tuple-element.7.base_ref, f32[768,512]{1,0:T(8,128)} %get-tuple-element.8.left_ref, bf16[2,768,128]{2,1,0:T(8,128)(2,1)} %get-tuple-element.9.out_ref, bf16[2,768,384]{2,1,0:T(8,128)(2,1)} %get-tuple-element.10.cross_ref, ...), custom_call_target="tpu_custom_call" | custom-call | tf_op jit(solution)/shard_map/pallas_call | solution.py:758

commit v4 on v3

--- a/solution.py
+++ b/solution.py
@@ -332,10 +332,9 @@
         begin(halo_in[0].up, halo_in[0].high)
         for copy in load_share:
             copy.wait()
-        begin(e1, halo_in[1].up, halo_in[1].high)
-        for k in range(2):
-            arrived(halo_in[k].low)
-            begin(halo_in[k].down)
+        begin(e1)
+        arrived(halo_in[0].low)
+        begin(halo_in[0].down)
 
     @on(0)
     def _():
@@ -353,7 +352,7 @@
     @on(1)
     def _():
         begin(e_core)
-        for piece in halo_in[2:]:
+        for piece in halo_in[1:]:
             begin(piece.up, piece.high)
             arrived(piece.low)
             begin(piece.down)
@@ -589,8 +588,6 @@
 
         lax.fori_loop(0, 2, side2, 0)
 
-    sides(0)
-
     r5 = message(block_own, block_out.at[half], mate_z, 0)
     r5_twin = message(block_own, block_out.at[half], twin, 0)
     r5_far = message(block_own, block_out.at[half], mate_z1, 0)
@@ -614,6 +611,7 @@
         begin(r5, r5_far, r5_twin, *extra)
         block_out[half] = block_own[...]
 
+    sides(0)
     sides(1)
     left_store = pltpu.make_async_copy(resid, left_o, store_sem.at[1])
     left_store.start()

time: 89 us -> 89.6 us (level); the launches traced: 88.8 us -> 87.9 us
  no operation moved by 1% of the time
where the time goes in v4:
time: 89.6 us; the launch traced here: 87.9 us
  Pallas kernels  87.3 us (97%)
    pallas_call x1, Pallas kernels, tree(): pl.pallas_call(tree_kernel, out_shape=[jax.ShapeDtypeStruct((LEAF, RHS),...  80.6 us
    pallas_call x1, Pallas kernels, tree(): pl.pallas_call(last_kernel, grid=(LEAF // block,), in_specs=[pl.BlockSpec...  6.66 us

profile of v4, /device:TPU:33, one launch (start us, length us, event | category | flops | bytes accessed | tf_op | source)
XLA Modules:
  0.0 87.9 jit_solution(3499928061009181273)
XLA Ops:
  0.6 80.6 %shard_map.122 = (f32[768,512]{1,0:T(8,128)}, f32[768,512]{1,0:T(8,128)}, bf16[2,768,128]{2,1,0:T(8,128)(2,1)}, bf16[2,768,384]{2,1,0:T(8,128)(2,1)}, bf16[2,384,512]{2,1,0:T(8,128)(2,1)}) custom-call(f32[768,512]{1,0:T(8,128)} %right_h.1, f32[768,512]{1,0:T(8,128)} %guess_h.1, f32[768,768]{1,0:T(8,128)} %bitcast.9, f32[768,768]{1,0:T(8,128)} %bitcast.10, ...), custom_call_target="tpu_custom_call" | custom-call | tf_op jit(solution)/shard_map/pallas_call | solution.py:739
  81.3 6.7 %shard_map.123 = (f32[768,512]{1,0:T(8,128)}, f32[768,512]{1,0:T(8,128)}) custom-call(f32[768,512]{1,0:T(8,128)} %get-tuple-element.7.base_ref, f32[768,512]{1,0:T(8,128)} %get-tuple-element.8.left_ref, bf16[2,768,128]{2,1,0:T(8,128)(2,1)} %get-tuple-element.9.out_ref, bf16[2,768,384]{2,1,0:T(8,128)(2,1)} %get-tuple-element.10.cross_ref, ...), custom_call_target="tpu_custom_call" | custom-call | tf_op jit(solution)/shard_map/pallas_call | solution.py:756

commit v5 on v2

--- a/solution.py
+++ b/solution.py
@@ -413,14 +413,14 @@
     reduce_chunk(0)
     base[:, cols(0)] = guess[:, cols(0)] + sol[:, cols(0)]
 
+    pump(1)
+    leaf_chunk(1)
+    reduce_chunk(1)
+    r1 = [remote(reduced.at[pl.ds(spots[d] * 128, 128)], r1_in.at[d], mates[d]) for d in range(3)]
+    pump(2)
     arrived(zq)
     group_m[3, half] = zq_out[...] + zq_in[...]
     g_half = remote(group_m.at[3, half], group_m.at[3, half], twin)
-
-    leaf_chunk(1)
-    reduce_chunk(1)
-    r1 = [remote(reduced.at[pl.ds(spots[d] * 128, 128)], r1_in.at[d], mates[d]) for d in range(3)]
-    pump(2)
     base[:, cols(1)] = guess[:, cols(1)] + sol[:, cols(1)]
     base_store = pltpu.make_async_copy(base, base_o, store_sem.at[0])
     base_store.start()
@@ -468,7 +468,7 @@
     root_rhs = u_out[...] + r3_in[0] + r3_in[1] + r3_in[2]
     gout[few_rows] = group_part + dot(root_rhs, down)
     r4 = [remote(gout.at[few_rows], gout.at[few_rows], peers[d]) for d in range(7)]
-    pump(2)
+    pump(1)
 
     def keep(ref, here, value):
         high, low = split(value)
@@ -640,7 +640,7 @@
             collective_id=0, has_side_effects=True, vmem_limit_bytes=56 * 2**20
         ),
     )(*args)
-    block = 128
+    block = 256
     return pl.pallas_call(
         last_kernel,
         grid=(LEAF // block,),

time: 86.8 us -> 84.9 us (0.978)
  Pallas kernels: 86 us -> 84.1 us
    pallas_call x1, Pallas kernels: 79.3 us -> 78.3 us  [tree(): pl.pallas_call(tree_kernel, out_shape=[jax.ShapeDtypeStruct((LEAF, RHS),...]
where the time goes in v5:
time: 84.9 us; the launch traced here: 84.8 us
  Pallas kernels  84.1 us (99%)
    pallas_call x1, Pallas kernels, tree(): pl.pallas_call(tree_kernel, out_shape=[jax.ShapeDtypeStruct((LEAF, RHS),...  78.3 us
    pallas_call x1, Pallas kernels, tree(): pl.pallas_call(last_kernel, grid=(LEAF // block,), in_specs=[pl.BlockSpec...  5.84 us

profile of v5, /device:TPU:33, one launch (start us, length us, event | category | flops | bytes accessed | tf_op | source)
XLA Modules:
  0.0 84.8 jit_solution(5481646065854561362)
XLA Ops:
  0.6 78.3 %shard_map.122 = (f32[768,512]{1,0:T(8,128)}, f32[768,512]{1,0:T(8,128)}, bf16[2,768,128]{2,1,0:T(8,128)(2,1)}, bf16[2,768,384]{2,1,0:T(8,128)(2,1)}, bf16[2,384,512]{2,1,0:T(8,128)(2,1)}) custom-call(f32[768,512]{1,0:T(8,128)} %right_h.1, f32[768,512]{1,0:T(8,128)} %guess_h.1, f32[768,768]{1,0:T(8,128)} %bitcast.9, f32[768,768]{1,0:T(8,128)} %bitcast.10, ...), custom_call_target="tpu_custom_call" | custom-call | tf_op jit(solution)/shard_map/pallas_call | solution.py:627
  78.9 5.8 %shard_map.123 = (f32[768,512]{1,0:T(8,128)}, f32[768,512]{1,0:T(8,128)}) custom-call(f32[768,512]{1,0:T(8,128)} %get-tuple-element.7.base_ref, f32[768,512]{1,0:T(8,128)} %get-tuple-element.8.left_ref, bf16[2,768,128]{2,1,0:T(8,128)(2,1)} %get-tuple-element.9.out_ref, bf16[2,768,384]{2,1,0:T(8,128)(2,1)} %get-tuple-element.10.cross_ref, ...), custom_call_target="tpu_custom_call" | custom-call | tf_op jit(solution)/shard_map/pallas_call | solution.py:644
